TPU v7x, 32 devices: a whole 2x2x4 slice. The times are simulated.
32 devices in a mesh: seq: 8 (over z, y), head: 4 (over x, core).
Axes of the slice: x: 2, y: 2, z: 4, core: 2. Of those that a mesh axis runs over, the one named last changes fastest.
Arguments:
- tokens: bfloat16 [12288, 3072], P('seq', 'head'), may hold values from -6 to 6
- w_qkv: bfloat16 [3072, 9216], P(None, 'head'), may hold values from -0.108253175 to 0.108253175
- w_out: bfloat16 [3072, 3072], P('head'), may hold values from -0.109375 to 0.109375
- dest_shard: int32 [6144, 1], replicated, may hold values from 0 to 7; in each aligned block of 768 rows (0 to 767, 768 to 1535, ...) at most 192 rows name the same one
- dest_index: int32 [6144], replicated, may hold values from 0 to 767
- merge_weight: bfloat16 [6144], replicated, may hold values from 0.25 to 2
- shift: float32 [3072], replicated, may hold values from -3 to 3
- scale: float32 [3072], replicated, may hold values from -0.5 to 0.5
- gate: float32 [3072], replicated, may hold values from 0.5 to 1.5
- q_gain: float32 [128], replicated, may hold values from 0.8 to 5
- k_gain: float32 [128], replicated, may hold values from 0.8 to 5
Outputs:
- result: bfloat16 [12288, 3072], P('seq', 'head')
Inputs may be any that keep to these rules, and one draw needn't show every extreme that they name: `dest_shard`: in each aligned block of 768 rows (the merged-away tokens of one shard) no shard is named more than 192 times, a bound that some block reaches.
All inputs are finite; a program needn't handle non-finite values.
Results may differ from a plain program's by a relative error of at most 0.015.
Values may be sent and summed in bfloat16 or wider, within the bound.
A program may use at most 320 MiB of HBM per device.

v0:
```python
import jax
import jax.numpy as jnp
from jax import lax
from jax.sharding import PartitionSpec as P

HD = 128


eps = 1e-06


def head_norm(values, gain):
    return values * lax.rsqrt(jnp.mean(values * values, axis=-1, keepdims=True) + eps) * gain


def body(
    tokens, w_qkv, w_out, dest_shard, dest_index, merge_weight, shift, scale, gate, q_gain, k_gain
):
    shards = lax.axis_size("seq")
    mine = lax.axis_index("seq")
    feature_part = lax.axis_index("head")
    rows, width = tokens.shape
    half = rows // 2
    capacity = max(2, 2 * half // shards)
    slots_all = shards * capacity
    owner = dest_shard[:, 0].reshape(shards, half)
    index = dest_index.reshape(shards, half)
    weight = merge_weight.astype(jnp.float32).reshape(shards, half)
    owner_hot = (owner[:, :, None] == jnp.arange(shards)[None, None, :]).astype(jnp.int32)
    rank = jnp.sum((jnp.cumsum(owner_hot, axis=1) - 1) * owner_hot, axis=2)
    slot = owner * capacity + rank
    my_slot = lax.dynamic_index_in_dim(slot, mine, 0, keepdims=False)
    packer = (jnp.arange(slots_all)[:, None] == my_slot[None, :]).astype(jnp.bfloat16)
    kept = tokens[:half]
    moved = tokens[half:]
    outgoing = jnp.dot(packer, moved, preferred_element_type=jnp.float32).astype(jnp.bfloat16)
    incoming = lax.all_to_all(
        outgoing.reshape(shards, capacity, width), "seq", split_axis=0, concat_axis=0, tiled=True
    )
    incoming = incoming.reshape(slots_all, width)
    chosen = (owner == mine)[:, :, None] & (rank[:, :, None] == jnp.arange(capacity)[None, None, :])
    slot_weight = jnp.sum(jnp.where(chosen, weight[:, :, None], 0.0), axis=1).reshape(slots_all)
    slot_index = jnp.sum(jnp.where(chosen, index[:, :, None], 0), axis=1).reshape(slots_all)
    slot_used = jnp.any(chosen, axis=1).reshape(slots_all)
    target_hot = (jnp.arange(half)[:, None] == slot_index[None, :]) & slot_used[None, :]
    spread = jnp.where(target_hot, slot_weight[None, :], 0.0)
    numer = kept.astype(jnp.float32) + jnp.dot(
        spread.astype(jnp.bfloat16), incoming, preferred_element_type=jnp.float32
    )
    denom = 1.0 + jnp.sum(spread, axis=1, keepdims=True)
    merged = (numer / denom).astype(jnp.bfloat16)
    qkv_cols = w_qkv.shape[1]
    merged_f = merged.astype(jnp.float32)
    row_total, row_squares = lax.psum(
        (jnp.sum(merged_f, axis=1), jnp.sum(merged_f * merged_f, axis=1)), "head"
    )
    features = width * lax.axis_size("head")
    mean = row_total / features
    var = row_squares / features - mean * mean
    scale_here = lax.dynamic_slice_in_dim(scale, feature_part * width, width)
    shift_here = lax.dynamic_slice_in_dim(shift, feature_part * width, width)
    normed = (
        (merged_f - mean[:, None]) * lax.rsqrt(var + eps)[:, None] * (1.0 + scale_here) + shift_here
    ).astype(jnp.bfloat16)
    qkv = jnp.dot(
        lax.all_gather(normed, "head", axis=1, tiled=True),
        w_qkv,
        preferred_element_type=jnp.float32,
    )
    heads_here = qkv_cols // (3 * HD)
    qkv = qkv.reshape(half, heads_here, 3, HD)
    query = head_norm(qkv[:, :, 0], q_gain).astype(jnp.bfloat16)
    keys = head_norm(qkv[:, :, 1], k_gain).astype(jnp.bfloat16).reshape(half, heads_here * HD)
    values = qkv[:, :, 2].astype(jnp.bfloat16).reshape(half, heads_here * HD)
    running_max = jnp.full((heads_here, half), -1e30, jnp.float32)
    running_sum = jnp.zeros((heads_here, half), jnp.float32)
    running_out = jnp.zeros((heads_here, half, HD), jnp.float32)
    key_piece = lax.all_gather(keys, "seq", axis=0, tiled=True)
    value_piece = lax.all_gather(values, "seq", axis=0, tiled=True)
    count = key_piece.shape[0]
    for lower in range(0, count, 1024):
        key_block = key_piece[lower : lower + 1024].reshape(-1, heads_here, HD)
        value_block = value_piece[lower : lower + 1024].reshape(-1, heads_here, HD)
        scores = jnp.einsum(
            "qhd,khd->hqk", query, key_block, preferred_element_type=jnp.float32
        ) * HD ** (-0.5)
        top = jnp.maximum(running_max, jnp.max(scores, axis=2))
        fade = jnp.exp(running_max - top)
        probs = jnp.exp(scores - top[:, :, None])
        running_sum = running_sum * fade + jnp.sum(probs, axis=2)
        running_out = running_out * fade[:, :, None] + jnp.einsum(
            "hqk,khd->hqd",
            probs.astype(jnp.bfloat16),
            value_block,
            preferred_element_type=jnp.float32,
        )
        running_max = top
    attended = (
        (running_out / running_sum[:, :, None])
        .transpose(1, 0, 2)
        .reshape(half, heads_here * HD)
        .astype(jnp.bfloat16)
    )
    share = lax.psum_scatter(
        lax.dot_general(
            w_out, attended, (((0,), (1,)), ((), ())), preferred_element_type=jnp.float32
        ).astype(jnp.bfloat16),
        "head",
        scatter_dimension=0,
        tiled=True,
    ).astype(jnp.float32)
    proj = share.T.astype(jnp.bfloat16)
    gate_here = lax.dynamic_slice_in_dim(gate, feature_part * width, width)
    kept_out = kept.astype(jnp.float32) + gate_here * proj.astype(jnp.float32)
    picker = ((jnp.arange(half)[None, :] == slot_index[:, None]) & slot_used[:, None]).astype(
        jnp.bfloat16
    )
    returning = jnp.dot(picker, proj, preferred_element_type=jnp.float32).astype(jnp.bfloat16)
    back = lax.all_to_all(
        returning.reshape(shards, capacity, width), "seq", split_axis=0, concat_axis=0, tiled=True
    ).reshape(slots_all, width)
    moved_proj = lax.dot_general(
        packer, back, (((0,), (0,)), ((), ())), preferred_element_type=jnp.float32
    )
    moved_out = moved.astype(jnp.float32) + gate_here * moved_proj
    return jnp.concatenate([kept_out, moved_out], axis=0).astype(jnp.bfloat16)


def solution(mesh):
    placed = (
        P("seq", "head"),
        P(None, "head"),
        P("head", None),
        P(),
        P(),
        P(),
        P(),
        P(),
        P(),
        P(),
        P(),
    )
    return jax.shard_map(
        body, mesh=mesh, in_specs=placed, out_specs=P("seq", "head"), check_vma=False
    )
```

profile of v0, /device:TPU:0, one launch (start us, length us, event | category | flops | bytes accessed | tf_op | source)
XLA Modules:
  0.0 684.6 jit_solution(1407470614389022784)
XLA Ops:
  9.3 13.5 %reduce-window.6 = s32[8,8,6,128]{3,1,2,0:T(8,128)S(1)} reduce-window(s32[8,8,6,128]{3,1,2,0:T(8,128)S(1)} %fusion.78, s32[]{:T(128)} %constant.20.clone.1), window={size=1x1x1x128 pad=0_0x0_0x0_0x127_0}, to_apply=%region_0.0 | reduce-window | flops 6242304 | bytes 393220 | tf_op jit(solution)/shard_map/reduce-window
  44.5 45.4 %all-to-all-done = bf16[8,192,768]{2,1,0:T(8,128)(2,1)} async-done(((bf16[8,192,768]{2,1,0:T(8,128)(2,1)}), bf16[8,192,768]{2,1,0:T(8,128)(2,1)}, u32[]{:S(2)}, u32[]{:S(2)}) %all-to-all-start) | async-done | bytes 2359328 | tf_op jit(solution)/shard_map/all_to_all | solution.py:37
  102.6 36.4 %all-gather.4.cloned.1.call-done = bf16[768,3072]{0,1:T(8,128)(2,1)} async-done(((bf16[768,768]{0,1:T(8,128)(2,1)}), bf16[768,3072]{0,1:T(8,128)(2,1)}) %all-gather.4.cloned.1.call-update) | async-done | bytes 4718608 | tf_op jit(solution)/shard_map/all_gather | solution.py:66
  139.0 16.1 %fusion.106 = f32[768,2304]{0,1:T(8,128)S(1)} fusion(bf16[768,3072]{0,1:T(8,128)(2,1)} %all-gather.4.cloned.1.call-done, bf16[3072,2304]{1,0:T(8,128)(2,1)} %param.12), kind=kOutput, calls=%fused_computation.163 | convolution fusion | flops 10871635968 | bytes 25952256 | tf_op jit(solution)/shard_map/dot_general | solution.py:65
  166.6 131.1 %all-gather.6.cloned.1.call-done = bf16[6144,768]{0,1:T(8,128)(2,1)} async-done(((bf16[768,768]{0,1:T(8,128)(2,1)}), bf16[6144,768]{0,1:T(8,128)(2,1)}) %all-gather.6.cloned.1.call-update) | async-done | bytes 9437200 | tf_op jit(solution)/shard_map/all_gather | solution.py:78
  302.0 8.6 %multiply_reduce_fusion.5 = (f32[6,768]{1,0:T(8,128)S(1)}, f32[6,768,1024]{2,1,0:T(8,128)}) fusion(bf16[768,6,128]{0,2,1:T(8,128)(2,1)S(1)} %multiply_convert_fusion, bf16[1024,6,128]{0,2,1:T(8,128)(2,1)S(1)} %bitcast.204), kind=kOutput, calls=%fused_computation.11 | convolution fusion | flops 1217392128 | bytes 21645312 | tf_op jit(solution)/shard_map/qhd,khd->hqk/dot_general | solution.py:84
  318.5 8.0 %multiply_reduce_fusion.4 = (f32[6,768]{1,0:T(8,128)S(1)}, f32[6,768,1024]{2,1,0:T(8,128)}) fusion(bf16[768,6,128]{0,2,1:T(8,128)(2,1)S(1)} %multiply_convert_fusion, bf16[1024,6,128]{0,2,1:T(8,128)(2,1)S(1)} %bitcast.202), kind=kOutput, calls=%fused_computation.10 | convolution fusion | flops 1217392128 | bytes 21645312 | tf_op jit(solution)/shard_map/qhd,khd->hqk/dot_general | solution.py:84
  326.4 8.0 %multiply_reduce_fusion = (f32[6,768]{1,0:T(8,128)S(1)}, f32[6,768,1024]{2,1,0:T(8,128)}) fusion(bf16[768,6,128]{0,2,1:T(8,128)(2,1)S(1)} %multiply_convert_fusion, bf16[1024,6,128]{0,2,1:T(8,128)(2,1)S(1)} %bitcast.201), kind=kOutput, calls=%fused_computation.6 | convolution fusion | flops 1217392128 | bytes 21645312 | tf_op jit(solution)/shard_map/qhd,khd->hqk/dot_general | solution.py:84
  350.3 10.9 %fusion.10 = f32[6,768]{1,0:T(8,128)S(1)} fusion(f32[6,768,1024]{2,1,0:T(8,128)} %get-tuple-element.43, f32[6,768]{1,0:T(8,128)S(1)} %get-tuple-element.14), kind=kLoop, calls=%fused_computation.22 | loop fusion | flops 14151168 | bytes 18911232 | tf_op jit(solution)/shard_map/reduce_sum | solution.py:90
  361.2 74.6 %all-gather.8.cloned.1.call-done = bf16[6144,768]{0,1:T(8,128)(2,1)} async-done(((bf16[768,768]{0,1:T(8,128)(2,1)}), bf16[6144,768]{0,1:T(8,128)(2,1)}) %all-gather.8.cloned.1.call-update) | async-done | bytes 9437200 | tf_op jit(solution)/shard_map/all_gather | solution.py:79
  441.9 9.3 %fusion.12 = f32[6,768,128]{1,2,0:T(8,128)} fusion(bf16[1024,6,128]{0,2,1:T(8,128)(2,1)S(1)} %bitcast.213, f32[6,768,1024]{2,1,0:T(8,128)} %get-tuple-element.43, f32[6,768]{1,0:T(8,128)S(1)} %get-tuple-element.14), kind=kOutput, calls=%fused_computation.24 | convolution fusion | flops 1222115328 | bytes 22824960 | tf_op jit(solution)/shard_map/hqk,khd->hqd/dot_general | solution.py:91
  451.2 9.8 %fusion.8 = f32[6,768]{1,0:T(8,128)S(1)} fusion(f32[6,768,1024]{2,1,0:T(8,128)} %get-tuple-element.45, f32[6,768]{1,0:T(8,128)S(1)} %get-tuple-element.15), kind=kLoop, calls=%fused_computation.20 | loop fusion | flops 14151168 | bytes 18911232 | tf_op jit(solution)/shard_map/reduce_sum | solution.py:90
  461.0 9.9 %fusion.14 = f32[6,768,128]{1,2,0:T(8,128)} fusion(bf16[1024,6,128]{0,2,1:T(8,128)(2,1)} %bitcast.212, f32[6,768,1024]{2,1,0:T(8,128)} %get-tuple-element.45, f32[6,768]{1,0:T(8,128)S(1)} %get-tuple-element.15), kind=kOutput, calls=%fused_computation.25 | convolution fusion | flops 1222115328 | bytes 22824960 | tf_op jit(solution)/shard_map/hqk,khd->hqd/dot_general | solution.py:91
  470.8 9.8 %fusion.6 = f32[6,768]{1,0:T(8,128)S(1)} fusion(f32[6,768,1024]{2,1,0:T(8,128)} %get-tuple-element.47, f32[6,768]{1,0:T(8,128)S(1)} %get-tuple-element.16), kind=kLoop, calls=%fused_computation.18 | loop fusion | flops 14151168 | bytes 18911232 | tf_op jit(solution)/shard_map/reduce_sum | solution.py:90
  480.6 9.7 %fusion.16 = f32[6,768,128]{1,2,0:T(8,128)} fusion(bf16[1024,6,128]{0,2,1:T(8,128)(2,1)} %bitcast.211, f32[6,768,1024]{2,1,0:T(8,128)} %get-tuple-element.47, f32[6,768]{1,0:T(8,128)S(1)} %get-tuple-element.16), kind=kOutput, calls=%fused_computation.26 | convolution fusion | flops 1222115328 | bytes 22824960 | tf_op jit(solution)/shard_map/hqk,khd->hqd/dot_general | solution.py:91
  490.4 9.8 %fusion.4 = f32[6,768]{1,0:T(8,128)S(1)} fusion(f32[6,768,1024]{2,1,0:T(8,128)} %get-tuple-element.49, f32[6,768]{1,0:T(8,128)S(1)} %get-tuple-element.17), kind=kLoop, calls=%fused_computation.16 | loop fusion | flops 14151168 | bytes 18911232 | tf_op jit(solution)/shard_map/reduce_sum | solution.py:90
  500.2 9.8 %fusion.18 = f32[6,768,128]{1,2,0:T(8,128)} fusion(bf16[1024,6,128]{0,2,1:T(8,128)(2,1)S(1)} %bitcast.210, f32[6,768,1024]{2,1,0:T(8,128)} %get-tuple-element.49, f32[6,768]{1,0:T(8,128)S(1)} %get-tuple-element.17), kind=kOutput, calls=%fused_computation.27 | convolution fusion | flops 1222115328 | bytes 22824960 | tf_op jit(solution)/shard_map/hqk,khd->hqd/dot_general | solution.py:91
  510.0 9.8 %fusion.2 = f32[6,768]{1,0:T(8,128)S(1)} fusion(f32[6,768,1024]{2,1,0:T(8,128)} %get-tuple-element.51, f32[6,768]{1,0:T(8,128)S(1)} %get-tuple-element.18), kind=kLoop, calls=%fused_computation.14 | loop fusion | flops 14151168 | bytes 18911232 | tf_op jit(solution)/shard_map/reduce_sum | solution.py:90
  519.8 9.3 %fusion.20 = f32[6,768,128]{1,2,0:T(8,128)} fusion(bf16[1024,6,128]{0,2,1:T(8,128)(2,1)S(1)} %bitcast.209, f32[6,768,1024]{2,1,0:T(8,128)} %get-tuple-element.51, f32[6,768]{1,0:T(8,128)S(1)} %get-tuple-element.18), kind=kOutput, calls=%fused_computation.28 | convolution fusion | flops 1222115328 | bytes 22824960 | tf_op jit(solution)/shard_map/hqk,khd->hqd/dot_general | solution.py:91
  529.1 9.9 %fusion = f32[6,768]{1,0:T(8,128)S(1)} fusion(f32[6,768,1024]{2,1,0:T(8,128)} %get-tuple-element.53, f32[6,768]{1,0:T(8,128)S(1)} %get-tuple-element.38), kind=kLoop, calls=%fused_computation.12 | loop fusion | flops 14151168 | bytes 18911232 | tf_op jit(solution)/shard_map/reduce_sum | solution.py:90
  539.1 11.8 %fusion.59 = bf16[768,6,128]{0,2,1:T(8,128)(2,1)S(1)} fusion(f32[6,768,128]{1,2,0:T(8,128)S(1)} %copy-done.6, f32[6,768,128]{1,2,0:T(8,128)} %fusion.14, f32[6,768,128]{1,2,0:T(8,128)} %fusion.16, f32[6,768,128]{1,2,0:T(8,128)} %fusion.18, f32[6,768,128]{1,2,0:T(8,128)} %fusion.20, bf16[1024,6,128]{0,2,1:T(8,128)(2,1)} %bitcast.216, ...), kind=kOutput, calls=%fused_computation.80 | convolution fusion | flops 1229783040 | bytes 33570816 | tf_op jit(solution)/shard_map/hqk,khd->hqd/dot_general | solution.py:91
  550.9 9.7 %fusion.44 = bf16[3072,768]{1,0:T(8,128)(2,1)} fusion(bf16[768,768]{0,1:T(8,128)(2,1)S(1)} %bitcast.218, bf16[768,3072]{1,0:T(8,128)(2,1)} %param.13), kind=kOutput, calls=%fused_computation.58 | convolution fusion | flops 3626237952 | bytes 10616832 | tf_op jit(solution)/shard_map/dot_general | solution.py:105
  560.6 46.1 %reduce-scatter.2.cloned.1.call-done = bf16[768,768]{1,0:T(8,128)(2,1)} async-done(((bf16[3072,768]{1,0:T(8,128)(2,1)}), bf16[768,768]{1,0:T(8,128)(2,1)}) %reduce-scatter.2.cloned.1.call-update) | async-done | bytes 1179664 | tf_op jit(solution)/shard_map/reduce_scatter | solution.py:104
  621.6 49.8 %all-to-all-done.1 = bf16[8,192,768]{2,1,0:T(8,128)(2,1)} async-done(((bf16[8,192,768]{2,1,0:T(8,128)(2,1)}), bf16[8,192,768]{2,1,0:T(8,128)(2,1)}, u32[]{:S(2)}, u32[]{:S(2)}) %all-to-all-start.1) | async-done | bytes 2359328 | tf_op jit(solution)/shard_map/all_to_all | solution.py:119
  (98 shorter events, 103.8 us)
Async XLA Ops:
  6.5 96.1 %copy-start = (f32[128]{0:T(128)S(1)}, f32[128]{0:T(128)}, u32[]{:S(2)}) copy-start(f32[128]{0:T(128)} %param.21) | copy-start | bytes 1540
  23.6 4.9 copy-start.14
  28.5 7.5 %copy-start.10 = (s32[6144]{0:T(1024)S(1)}, s32[6144]{0:T(1024)}, u32[]{:S(2)}) copy-start(s32[6144]{0:T(1024)} %param.15) | copy-start | bytes 73732
  28.5 7.5 %copy-start.11 = (bf16[6144]{0:T(1024)(128)(2,1)S(1)}, bf16[6144]{0:T(1024)(128)(2,1)}, u32[]{:S(2)}) copy-start(bf16[6144]{0:T(1024)(128)(2,1)} %param.16) | copy-start | bytes 36868
  28.5 61.4 %all-to-all-start = ((bf16[8,192,768]{2,1,0:T(8,128)(2,1)}), bf16[8,192,768]{2,1,0:T(8,128)(2,1)}, u32[]{:S(2)}, u32[]{:S(2)}) async-start(bf16[8,192,768]{2,1,0:T(8,128)(2,1)} %bitcast.3), calls=%async_computation | async-start | bytes 4718592 | tf_op jit(solution)/shard_map/all_to_all | solution.py:37
  36.0 103.1 %all-gather.4.cloned.1.call-start = ((), (), s32[]{:S(2)}) async-start(), calls=%async_computation.3 | async-start | bytes 5898240 | tf_op jit(solution)/shard_map/all_gather | solution.py:66
  37.0 53.0 %copy-start.12 = (pred[1536]{0:T(1024)(128)(4,1)}, pred[1536]{0:T(1024)(128)(4,1)S(1)}, u32[]{:S(2)}) copy-start(pred[1536]{0:T(1024)(128)(4,1)S(1)} %and.30) | copy-start | bytes 4612
  38.1 51.8 %copy-start.8 = (s32[1536]{0:T(1024)}, s32[1536]{0:T(1024)S(1)}, u32[]{:S(2)}) copy-start(s32[1536]{0:T(1024)S(1)} %eq.102) | copy-start | bytes 18436
  42.7 51.3 %copy-start.3 = (bf16[768,768]{0,1:T(8,128)(2,1)}, bf16[768,768]{0,1:T(8,128)(2,1)S(1)}, u32[]{:S(2)}) copy-start(bf16[768,768]{0,1:T(8,128)(2,1)S(1)} %copy.75) | copy-start | bytes 3538948
  102.1 195.6 %all-gather.6.cloned.1.call-start = ((), (), s32[]{:S(2)}) async-start(), calls=%async_computation.4 | async-start | bytes 10616832 | tf_op jit(solution)/shard_map/all_gather | solution.py:78
  155.2 2.8 copy-start.2
  159.7 276.1 %all-gather.8.cloned.1.call-start = ((), (), s32[]{:S(2)}) async-start(), calls=%async_computation.5 | async-start | bytes 10616832 | tf_op jit(solution)/shard_map/all_gather | solution.py:79
  162.6 2.0 copy-start.16
  162.6 444.1 %reduce-scatter.2.cloned.1.call-start = ((), (), s32[]{:S(2)}) async-start(), calls=%async_computation.6 | async-start | bytes 5898240 | tf_op jit(solution)/shard_map/reduce_scatter | solution.py:104
  529.1 10.0 %copy-start.6 = (f32[6,768,128]{1,2,0:T(8,128)S(1)}, f32[6,768,128]{1,2,0:T(8,128)}, u32[]{:S(2)}) copy-start(f32[6,768,128]{1,2,0:T(8,128)} %fusion.12) | copy-start | bytes 7077892
  560.6 46.2 %copy-start.9 = (s32[1536]{0:T(1024)S(1)}, s32[1536]{0:T(1024)}, u32[]{:S(2)}) copy-start(s32[1536]{0:T(1024)} %copy-done.8) | copy-start | bytes 18436
  560.6 46.2 %copy-start.13 = (pred[1536]{0:T(1024)(128)(4,1)S(1)}, pred[1536]{0:T(1024)(128)(4,1)}, u32[]{:S(2)}) copy-start(pred[1536]{0:T(1024)(128)(4,1)} %copy-done.12) | copy-start | bytes 4612
  611.8 6.5 copy-start.5
  611.8 59.6 %all-to-all-start.1 = ((bf16[8,192,768]{2,1,0:T(8,128)(2,1)}), bf16[8,192,768]{2,1,0:T(8,128)(2,1)}, u32[]{:S(2)}, u32[]{:S(2)}) async-start(bf16[8,192,768]{2,1,0:T(8,128)(2,1)} %bitcast.215), calls=%async_computation.2 | async-start | bytes 4718592 | tf_op jit(solution)/shard_map/all_to_all | solution.py:119
  617.4 2.3 copy-start.4
  619.8 51.6 %copy-start.7 = (bf16[768,768]{0,1:T(8,128)(2,1)S(1)}, bf16[768,768]{0,1:T(8,128)(2,1)}, u32[]{:S(2)}) copy-start(bf16[768,768]{0,1:T(8,128)(2,1)} %copy.76) | copy-start | bytes 3538948
  619.8 51.6 %copy-start.15 = (s32[768]{0:T(1024)S(1)}, s32[768]{0:T(1024)}, u32[]{:S(2)}) copy-start(s32[768]{0:T(1024)} %copy-done.14) | copy-start | bytes 9220
  675.3 2.6 copy-start.1
Sparse Core Ops, SparseCore 0:
  102.2 36.7 all-gather.3
  159.9 137.7 all-gather.5
  299.8 135.9 all-gather.7
  560.7 45.9 reduce-scatter.1
where the time goes:
time: 693 us; the launch traced here: 685 us
  waiting for transfers between devices  383 us (55%)
  matrix products  152 us (22%)
  other arithmetic  89.2 us (13%)
  local copies, waits for them, and re-layouts  27.1 us (4%)
  starting transfers between devices  13.7 us (2%)
  between operations  13.7 us (2%)
    all_gather x1, waiting for transfers between devices, body(): key_piece = lax.all_gather(keys, 'seq', axis=0, tiled=True)  131 us
    all_gather x1, waiting for transfers between devices, body(): value_piece = lax.all_gather(values, 'seq', axis=0, tiled=True)  74.6 us
    reduce_sum x6, other arithmetic, body(): running_sum = running_sum * fade + jnp.sum(probs, axis=2)  60.1 us
    dot_general x6, matrix products, body(): jnp.einsum('hqk,khd->hqd', probs.astype(jnp.bfloat16), value_block, prefe...  59.8 us
    all_to_all x1, waiting for transfers between devices, body(): lax.all_to_all(returning.reshape(shards, capacity, width), 'seq', split_a...  49.8 us
    dot_general x6, matrix products, body(): jnp.einsum('qhd,khd->hqk', query, key_block, preferred_element_type=jnp.f...  48.3 us
    reduce_scatter x1, waiting for transfers between devices, body(): lax.psum_scatter(lax.dot_general(w_out, attended, (((0,), (1,)), ((), ())...  46.1 us
    all_to_all x1, waiting for transfers between devices, body(): lax.all_to_all(outgoing.reshape(shards, capacity, width), 'seq', split_ax...  45.4 us
  transfers between devices with their start and end apart: 6, of which 6 were waited for; matrix products, arithmetic and copies ran while one was open for 12% of the time, Pallas kernels for 0%

commit v1 on v0

v1 whole, which is shorter than its diff:
```python
import functools
import math

import jax
import jax.numpy as jnp
from jax import lax
from jax.experimental import pallas as pl
from jax.experimental.pallas import tpu as pltpu
from jax.sharding import PartitionSpec as P

HD = 128
eps = 1e-06
VMEM_BYTES = 50 * 1024 * 1024


def qkv_kernel(parts, group, x_ref, w_ref, scale_ref, shift_ref, qg_ref, kg_ref, q_ref, k_ref, v_ref, normed_ref):
    half, width = x_ref.shape[1], x_ref.shape[2]
    features = parts * width
    tile = 256

    @pl.when(pl.program_id(0) == 0)
    def _():
        def rows_step(i, carry):
            rows = pl.ds(pl.multiple_of(i * tile, tile), tile)
            total = jnp.zeros((tile, 1), jnp.float32)
            squares = jnp.zeros((tile, 1), jnp.float32)
            for j in range(parts):
                x = x_ref[j, rows, :].astype(jnp.float32)
                total += jnp.sum(x, axis=1, keepdims=True)
                squares += jnp.sum(x * x, axis=1, keepdims=True)
            mean = total / features
            inv = lax.rsqrt(squares / features - mean * mean + eps)
            for j in range(parts):
                cols = slice(j * width, (j + 1) * width)
                x = x_ref[j, rows, :].astype(jnp.float32)
                normed_ref[rows, cols] = (
                    (x - mean) * inv * (1.0 + scale_ref[:, cols]) + shift_ref[:, cols]
                ).astype(jnp.bfloat16)
            return carry

        lax.fori_loop(0, half // tile, rows_step, 0)

    def norm(values, gain):
        return values * lax.rsqrt(jnp.mean(values * values, axis=-1, keepdims=True) + eps) * gain

    def out_step(i, carry):
        rows = pl.ds(pl.multiple_of(i * tile, tile), tile)
        out = jnp.dot(normed_ref[rows, :], w_ref[...], preferred_element_type=jnp.float32)
        for g in range(group):
            base = g * 3 * HD
            cols = slice(g * HD, (g + 1) * HD)
            q_ref[rows, cols] = norm(out[:, base : base + HD], qg_ref[...]).astype(jnp.bfloat16)
            k_ref[rows, cols] = norm(out[:, base + HD : base + 2 * HD], kg_ref[...]).astype(jnp.bfloat16)
            v_ref[rows, cols] = out[:, base + 2 * HD : base + 3 * HD].astype(jnp.bfloat16)
        return carry

    lax.fori_loop(0, half // tile, out_step, 0)


def project_qkv(gathered, w_qkv, scale, shift, q_gain, k_gain):
    parts, half, width = gathered.shape
    depth, cols = w_qkv.shape
    heads = cols // (3 * HD)
    group = 2 if heads % 2 == 0 else 1
    whole = lambda shape: pl.BlockSpec(shape, lambda i: (0,) * len(shape))
    out = jax.ShapeDtypeStruct((half, heads * HD), jnp.bfloat16)
    return pl.pallas_call(
        functools.partial(qkv_kernel, parts, group),
        grid=(heads // group,),
        in_specs=[
            whole((parts, half, width)),
            pl.BlockSpec((depth, group * 3 * HD), lambda i: (0, i)),
            whole((1, depth)),
            whole((1, depth)),
            whole((1, HD)),
            whole((1, HD)),
        ],
        out_specs=[pl.BlockSpec((half, group * HD), lambda i: (0, i))] * 3,
        out_shape=[out] * 3,
        scratch_shapes=[pltpu.VMEM((half, depth), jnp.bfloat16)],
        compiler_params=pltpu.CompilerParams(
            dimension_semantics=("arbitrary",), vmem_limit_bytes=VMEM_BYTES
        ),
        cost_estimate=pl.CostEstimate(
            flops=2 * half * depth * cols, bytes_accessed=2 * depth * cols + 8 * half * depth, transcendentals=0
        ),
    )(gathered, w_qkv, scale[None, :], shift[None, :], q_gain[None, :], k_gain[None, :])


def flash_kernel(blocks, first, last, *refs):
    q_ref = refs[0]
    k_refs = refs[1 : 1 + blocks]
    v_refs = refs[1 + blocks : 1 + 2 * blocks]
    rest = refs[1 + 2 * blocks :]
    factor = HD ** (-0.5) * math.log2(math.e)
    q = q_ref[...]
    scores = [
        lax.dot_general(q, k[...], (((1,), (1,)), ((), ())), preferred_element_type=jnp.float32) for k in k_refs
    ]
    top = functools.reduce(jnp.maximum, [jnp.max(s, axis=1, keepdims=True) for s in scores])
    if not first:
        old = rest[0][:, :1]
        top = jnp.maximum(top, old)
    total = None
    for s, v in zip(scores, v_refs):
        probs = jnp.exp2((s - top) * factor).astype(jnp.bfloat16)
        values = jnp.concatenate([v[...], jnp.ones_like(v)], axis=1)
        term = jnp.dot(probs, values, preferred_element_type=jnp.float32)
        total = term if total is None else total + term
    if not first:
        total = total + rest[1][...] * jnp.exp2((old - top) * factor)
        rest = rest[2:]
    if last:
        rest[0][...] = (total[:, :HD] / total[:, HD:]).astype(jnp.bfloat16)
    else:
        rest[0][...] = jnp.broadcast_to(top, rest[0].shape)
        rest[1][...] = total


def flash(query, keys, values, state, last):
    rows, width = query.shape
    heads = width // HD
    blocks = len(keys)
    count = keys[0].shape[0]
    tile = 256
    first = state is None
    row_spec = pl.BlockSpec((tile, HD), lambda h, i: (i, h))
    acc_spec = pl.BlockSpec((tile, 2 * HD), lambda h, i: (i, h))
    key_spec = pl.BlockSpec((count, HD), lambda h, i: (0, h))
    state_specs = [row_spec, acc_spec]
    state_shapes = [
        jax.ShapeDtypeStruct((rows, width), jnp.float32),
        jax.ShapeDtypeStruct((rows, 2 * width), jnp.float32),
    ]
    state = () if first else tuple(state)
    return pl.pallas_call(
        functools.partial(flash_kernel, blocks, first, last),
        grid=(heads, rows // tile),
        in_specs=[row_spec] + [key_spec] * (2 * blocks) + ([] if first else state_specs),
        out_specs=row_spec if last else state_specs,
        out_shape=jax.ShapeDtypeStruct((rows, width), jnp.bfloat16) if last else state_shapes,
        compiler_params=pltpu.CompilerParams(
            dimension_semantics=("arbitrary", "arbitrary"), vmem_limit_bytes=VMEM_BYTES
        ),
        cost_estimate=pl.CostEstimate(
            flops=8 * rows * count * blocks * width,
            bytes_accessed=4 * count * blocks * width + 16 * rows * width,
            transcendentals=rows * count * blocks * heads,
        ),
    )(query, *keys, *values, *state)


def ring_pairs(shards):
    depth = 4 if shards % 8 == 0 else 1
    across = shards // depth
    order = []
    for y in range(across):
        line = range(depth) if y % 2 == 0 else range(depth - 1, -1, -1)
        order += [z * across + y for z in line]
    right = [(order[i], order[(i + 1) % shards]) for i in range(shards)]
    return right, [(b, a) for a, b in right]


def attend(query, keys, values):
    shards = lax.axis_size("seq")
    right, left = ring_pairs(shards)
    move_right = lambda x: lax.ppermute(x, "seq", right)
    move_left = lambda x: lax.ppermute(x, "seq", left)
    fk, fv, bk, bv = keys, values, keys, values
    state = None
    here_k, here_v = [keys], [values]
    for step in range(1, shards // 2):
        fk, bk, fv, bv = move_right(fk), move_left(bk), move_right(fv), move_left(bv)
        state = flash(query, here_k, here_v, state, False)
        here_k, here_v = [fk, bk], [fv, bv]
    fk, bv = move_right(fk), move_left(bv)
    state = flash(query, here_k, here_v, state, False)
    return flash(query, [fk], [bv], state, True)


def body(
    tokens, w_qkv, w_out, dest_shard, dest_index, merge_weight, shift, scale, gate, q_gain, k_gain
):
    shards = lax.axis_size("seq")
    mine = lax.axis_index("seq")
    feature_part = lax.axis_index("head")
    rows, width = tokens.shape
    half = rows // 2
    capacity = max(2, 2 * half // shards)
    slots_all = shards * capacity
    owner = dest_shard[:, 0].reshape(shards, half)
    index = dest_index.reshape(shards, half)
    weight = merge_weight.astype(jnp.float32).reshape(shards, half)
    my_owner = lax.dynamic_index_in_dim(owner, mine, 0, keepdims=False)
    hot = jnp.concatenate(
        [my_owner[None, :] == jnp.arange(shards)[:, None], owner == mine], axis=0
    ).astype(jnp.bfloat16)
    upper = (jnp.arange(half)[:, None] <= jnp.arange(half)[None, :]).astype(jnp.bfloat16)
    place = jnp.dot(hot, upper, preferred_element_type=jnp.float32).astype(jnp.int32) - 1
    my_rank = jnp.sum(jnp.where(hot[:shards] > 0, place[:shards], 0), axis=0)
    my_slot = my_owner * capacity + my_rank
    rank = place[shards:]
    packer = (jnp.arange(slots_all)[:, None] == my_slot[None, :]).astype(jnp.bfloat16)
    kept = tokens[:half]
    moved = tokens[half:]
    outgoing = jnp.dot(packer, moved, preferred_element_type=jnp.float32).astype(jnp.bfloat16)
    incoming = lax.all_to_all(
        outgoing.reshape(shards, capacity, width), "seq", split_axis=0, concat_axis=0, tiled=True
    )
    incoming = incoming.reshape(slots_all, width)
    chosen = (owner == mine)[:, :, None] & (rank[:, :, None] == jnp.arange(capacity)[None, None, :])
    slot_weight = jnp.sum(jnp.where(chosen, weight[:, :, None], 0.0), axis=1).reshape(slots_all)
    slot_index = jnp.sum(jnp.where(chosen, index[:, :, None], 0), axis=1).reshape(slots_all)
    slot_used = jnp.any(chosen, axis=1).reshape(slots_all)
    target_hot = (jnp.arange(half)[:, None] == slot_index[None, :]) & slot_used[None, :]
    spread = jnp.where(target_hot, slot_weight[None, :], 0.0)
    numer = kept.astype(jnp.float32) + jnp.dot(
        spread.astype(jnp.bfloat16), incoming, preferred_element_type=jnp.float32
    )
    denom = 1.0 + jnp.sum(spread, axis=1, keepdims=True)
    merged = (numer / denom).astype(jnp.bfloat16)
    gathered = lax.all_gather(merged, "head", axis=0, tiled=False)
    query, keys, values = project_qkv(gathered, w_qkv, scale, shift, q_gain, k_gain)
    attended = attend(query, keys, values)
    share = lax.psum_scatter(
        lax.dot_general(
            w_out, attended, (((0,), (1,)), ((), ())), preferred_element_type=jnp.float32
        ).astype(jnp.bfloat16),
        "head",
        scatter_dimension=0,
        tiled=True,
    ).astype(jnp.float32)
    proj = share.T.astype(jnp.bfloat16)
    gate_here = lax.dynamic_slice_in_dim(gate, feature_part * width, width)
    kept_out = kept.astype(jnp.float32) + gate_here * proj.astype(jnp.float32)
    picker = ((jnp.arange(half)[None, :] == slot_index[:, None]) & slot_used[:, None]).astype(
        jnp.bfloat16
    )
    returning = jnp.dot(picker, proj, preferred_element_type=jnp.float32).astype(jnp.bfloat16)
    back = lax.all_to_all(
        returning.reshape(shards, capacity, width), "seq", split_axis=0, concat_axis=0, tiled=True
    ).reshape(slots_all, width)
    moved_proj = lax.dot_general(
        packer, back, (((0,), (0,)), ((), ())), preferred_element_type=jnp.float32
    )
    moved_out = moved.astype(jnp.float32) + gate_here * moved_proj
    return jnp.concatenate([kept_out, moved_out], axis=0).astype(jnp.bfloat16)


def solution(mesh):
    placed = (
        P("seq", "head"),
        P(None, "head"),
        P("head", None),
        P(),
        P(),
        P(),
        P(),
        P(),
        P(),
        P(),
        P(),
    )
    return jax.shard_map(
        body, mesh=mesh, in_specs=placed, out_specs=P("seq", "head"), check_vma=False
    )
```

time: 693 us -> 476 us (0.69); the launches traced: 685 us -> 475 us
  Pallas kernels: 0 us -> 133 us
  matrix products: 152 us -> 24 us
  waiting for transfers between devices: 383 us -> 266 us
  other arithmetic: 89.2 us -> 8.9 us
  local copies, waits for them, and re-layouts: 27.1 us -> 2.64 us
  starting transfers between devices: 13.7 us -> 27.3 us
    all_gather x3 -> x1, waiting for transfers between devices: 242 us -> 36.6 us  [body(): gathered = lax.all_gather(merged, 'head', axis=0, tiled=False)]
    pallas_call x0 -> x6, Pallas kernels: none -> 133 us  [the longest x5 112 us: flash(): pl.pallas_call(functools.partial(flash_kernel, blocks, first, last), grid...]
    dot_general x13 -> x1, matrix products: 124 us -> 0.22 us  [body(): jnp.dot(hot, upper, preferred_element_type=jnp.float32).astype(jnp.int32)]
    ppermute x0 -> x14, waiting for transfers between devices: none -> 81.6 us  [the longest x7 46.5 us: attend(): move_right = lambda x: lax.ppermute(x, 'seq', right)]
    reduce_sum x9 -> x1, other arithmetic: 62.4 us -> 0.02 us  [body(): my_rank = jnp.sum(jnp.where(hot[:shards] > 0, place[:shards], 0), axis=0)]
    slice x6 -> x0, local copies, waits for them, and re-layouts: 16.4 us -> none  [the longest x1 6.07 us: body(): value_block = value_piece[lower:lower + 1024].reshape(-1, heads_here, HD)]
    ppermute x0 -> x14, starting transfers between devices: none -> 14.3 us  [the longest x7 9.56 us: attend(): move_right = lambda x: lax.ppermute(x, 'seq', right)]
    another operation x3 -> x1, other arithmetic: 15.5 us -> 1.97 us
  transfers between devices with their start and end apart: 6 -> 18, of which waited for: 6 -> 8; matrix products, arithmetic and copies ran while one was open for 12% -> 1% of each run, Pallas kernels for 0% -> 20%
where the time goes in v1:
time: 476 us; the launch traced here: 475 us
  waiting for transfers between devices  266 us (56%)
  Pallas kernels  133 us (28%)
  starting transfers between devices  27.3 us (6%)
  matrix products  24 us (5%)
  between operations  13.6 us (3%)
  other arithmetic  8.9 us (2%)
    pallas_call x5, Pallas kernels, flash(): pl.pallas_call(functools.partial(flash_kernel, blocks, first, last), grid...  112 us
    all_to_all x1, waiting for transfers between devices, body(): lax.all_to_all(returning.reshape(shards, capacity, width), 'seq', split_a...  51.1 us
    all_to_all x1, waiting for transfers between devices, body(): lax.all_to_all(outgoing.reshape(shards, capacity, width), 'seq', split_ax...  49.6 us
    reduce_scatter x1, waiting for transfers between devices, body(): lax.psum_scatter(lax.dot_general(w_out, attended, (((0,), (1,)), ((), ())...  47.1 us
    ppermute x7, waiting for transfers between devices, attend(): move_right = lambda x: lax.ppermute(x, 'seq', right)  46.5 us
    all_gather x1, waiting for transfers between devices, body(): gathered = lax.all_gather(merged, 'head', axis=0, tiled=False)  36.6 us
    ppermute x7, waiting for transfers between devices, attend(): move_left = lambda x: lax.ppermute(x, 'seq', left)  35.2 us
    pallas_call x1, Pallas kernels, project_qkv(): pl.pallas_call(functools.partial(qkv_kernel, parts, group), grid=(heads /...  21 us
  transfers between devices with their start and end apart: 18, of which 8 were waited for; matrix products, arithmetic and copies ran while one was open for 1% of the time, Pallas kernels for 20%

profile of v1, /device:TPU:0, one launch (start us, length us, event | category | flops | bytes accessed | tf_op | source)
XLA Modules:
  0.0 475.5 jit_solution(5156595128392729625)
XLA Ops:
  8.8 4.9 %fusion.9 = bf16[1536,768]{1,0:T(8,128)(2,1)} fusion(s32[768]{0:T(1024)S(1)} %add_reduce_fusion, bf16[1536,768]{1,0:T(8,128)(2,1)} %param.11), kind=kOutput, calls=%fused_computation.17 | convolution fusion | flops 1814298624 | bytes 3542016 | tf_op jit(solution)/shard_map/dot_general | solution.py:206
  13.7 7.4 %all-to-all-start = ((bf16[8,192,768]{2,1,0:T(8,128)(2,1)}), bf16[8,192,768]{2,1,0:T(8,128)(2,1)S(1)}, u32[]{:S(2)}, u32[]{:S(2)}) async-start(bf16[8,192,768]{2,1,0:T(8,128)(2,1)} %bitcast.26), calls=%async_computation | async-start | bytes 4718592 | tf_op jit(solution)/shard_map/all_to_all | solution.py:207
  25.4 49.6 %all-to-all-done = bf16[8,192,768]{2,1,0:T(8,128)(2,1)S(1)} async-done(((bf16[8,192,768]{2,1,0:T(8,128)(2,1)}), bf16[8,192,768]{2,1,0:T(8,128)(2,1)S(1)}, u32[]{:S(2)}, u32[]{:S(2)}) %all-to-all-start) | async-done | bytes 2359328 | tf_op jit(solution)/shard_map/all_to_all | solution.py:207
  75.0 4.7 fusion.14
  79.7 36.6 %all-gather.3.cloned.1.call-done = bf16[3072,768]{1,0:T(8,128)(2,1)} async-done(((bf16[768,768]{1,0:T(8,128)(2,1)}), bf16[3072,768]{1,0:T(8,128)(2,1)}) %all-gather.3.cloned.1.call-update) | async-done | bytes 4718608 | tf_op jit(solution)/shard_map/all_gather | solution.py:222
  116.4 21.0 %shard_map.109 = (bf16[768,768]{1,0:T(8,128)(2,1)S(1)}, bf16[768,768]{1,0:T(8,128)(2,1)S(1)}, bf16[768,768]{1,0:T(8,128)(2,1)S(1)}) custom-call(bf16[4,768,768]{2,1,0:T(8,128)(2,1)} %bitcast.29, bf16[3072,2304]{1,0:T(8,128)(2,1)} %w_ref.1, f32[1,3072]{1,0:T(1,128)S(1)} %bitcast.19, f32[1,3072]{1,0:T(1,128)S(1)} %bitcast.20, f32[1,128]{1,0:T(1,128)S(1)} %bitcast.21, ...), custom_call_target="tpu_custom_call" | custom-call | flops 10871635968 | bytes 33030144 | tf_op jit(solution)/shard_map/pallas_call | solution.py:67
  137.4 1.5 collective-permute-start
  141.5 24.7 %collective-permute-done.refs_1_ = bf16[768,768]{1,0:T(8,128)(2,1)S(1)} collective-permute-done((bf16[768,768]{1,0:T(8,128)(2,1)S(1)}, bf16[768,768]{1,0:T(8,128)(2,1)S(1)}, u32[]{:S(2)}, u32[]{:S(2)}) %collective-permute-start) | collective-permute-done | bytes 1179680 | tf_op jit(solution)/shard_map/ppermute | solution.py:167
  168.3 24.7 %collective-permute-done.8.refs_2_ = bf16[768,768]{1,0:T(8,128)(2,1)S(1)} collective-permute-done((bf16[768,768]{1,0:T(8,128)(2,1)S(1)}, bf16[768,768]{1,0:T(8,128)(2,1)S(1)}, u32[]{:S(2)}, u32[]{:S(2)}) %collective-permute-start.8) | collective-permute-done | bytes 1179680 | tf_op jit(solution)/shard_map/ppermute | solution.py:168
  195.0 21.7 %collective-permute-done.1.refs_1_ = bf16[768,768]{1,0:T(8,128)(2,1)S(1)} collective-permute-done((bf16[768,768]{1,0:T(8,128)(2,1)S(1)}, bf16[768,768]{1,0:T(8,128)(2,1)S(1)}, u32[]{:S(2)}, u32[]{:S(2)}) %collective-permute-start.1) | collective-permute-done | bytes 1179680 | tf_op jit(solution)/shard_map/ppermute | solution.py:167
  218.8 14.4 %shard_map.110 = (f32[768,768]{1,0:T(8,128)}, f32[768,1536]{1,0:T(8,128)}) custom-call(bf16[768,768]{1,0:T(8,128)(2,1)S(1)} %get-tuple-element.16.refs_0_, bf16[768,768]{1,0:T(8,128)(2,1)S(1)} %get-tuple-element.17.refs_1_, bf16[768,768]{1,0:T(8,128)(2,1)S(1)} %get-tuple-element.18.refs_2_), custom_call_target="tpu_custom_call" | custom-call | flops 3623878656 | bytes 11796480 | tf_op jit(solution)/shard_map/pallas_call | solution.py:136
  233.2 10.3 %collective-permute-done.9.refs_2_ = bf16[768,768]{1,0:T(8,128)(2,1)S(1)} collective-permute-done((bf16[768,768]{1,0:T(8,128)(2,1)S(1)}, bf16[768,768]{1,0:T(8,128)(2,1)S(1)}, u32[]{:S(2)}, u32[]{:S(2)}) %collective-permute-start.9) | collective-permute-done | bytes 1179680 | tf_op jit(solution)/shard_map/ppermute | solution.py:168
  245.6 26.2 %shard_map.111 = (f32[768,768]{1,0:T(8,128)}, f32[768,1536]{1,0:T(8,128)}) custom-call(bf16[768,768]{1,0:T(8,128)(2,1)S(1)} %get-tuple-element.16.refs_0_, bf16[768,768]{1,0:T(8,128)(2,1)S(1)} %collective-permute-done.refs_1_, bf16[768,768]{1,0:T(8,128)(2,1)S(1)} %collective-permute-done.8.refs_2_, bf16[768,768]{1,0:T(8,128)(2,1)} %copy-done.8, ...), custom_call_target="tpu_custom_call" | custom-call | flops 7247757312 | bytes 14155776 | tf_op jit(solution)/shard_map/pallas_call | solution.py:136
  273.9 26.3 %shard_map.112 = (f32[768,768]{1,0:T(8,128)}, f32[768,1536]{1,0:T(8,128)}) custom-call(bf16[768,768]{1,0:T(8,128)(2,1)S(1)} %get-tuple-element.16.refs_0_, bf16[768,768]{1,0:T(8,128)(2,1)S(1)} %collective-permute-done.1.refs_1_, bf16[768,768]{1,0:T(8,128)(2,1)S(1)} %collective-permute-done.9.refs_2_, bf16[768,768]{1,0:T(8,128)(2,1)} %collective-permute-done.12.refs_3_, ...), custom_call_target="tpu_custom_call" | custom-call | flops 7247757312 | bytes 14155776 | tf_op jit(solution)/shard_map/pallas_call | solution.py:136
  300.2 26.2 %shard_map.113 = (f32[768,768]{1,0:T(8,128)}, f32[768,1536]{1,0:T(8,128)}) custom-call(bf16[768,768]{1,0:T(8,128)(2,1)S(1)} %get-tuple-element.16.refs_0_, bf16[768,768]{1,0:T(8,128)(2,1)S(1)} %collective-permute-done.2.refs_1_, bf16[768,768]{1,0:T(8,128)(2,1)S(1)} %collective-permute-done.10.refs_2_, bf16[768,768]{1,0:T(8,128)(2,1)} %collective-permute-done.13.refs_3_, ...), custom_call_target="tpu_custom_call" | custom-call | flops 7247757312 | bytes 14155776 | tf_op jit(solution)/shard_map/pallas_call | solution.py:136
  327.5 18.8 %shard_map.114 = bf16[768,768]{1,0:T(8,128)(2,1)S(1)} custom-call(bf16[768,768]{1,0:T(8,128)(2,1)S(1)} %get-tuple-element.16.refs_0_, bf16[768,768]{1,0:T(8,128)(2,1)S(1)} %collective-permute-done.3.refs_1_, bf16[768,768]{1,0:T(8,128)(2,1)} %copy-done.9, f32[768,768]{1,0:T(8,128)} %get-tuple-element.25.refs_3_, f32[768,1536]{1,0:T(8,128)} %get-tuple-element.26.refs_4_), custom_call_target="tpu_custom_call" | custom-call | flops 3623878656 | bytes 11796480 | tf_op jit(solution)/shard_map/pallas_call | solution.py:136
  346.3 5.6 %fusion.8 = bf16[3072,768]{0,1:T(8,128)(2,1)} fusion(bf16[768,768]{1,0:T(8,128)(2,1)S(1)} %shard_map.114, bf16[768,3072]{1,0:T(8,128)(2,1)S(1)} %bitcast.28), kind=kOutput, calls=%fused_computation.16 | convolution fusion | flops 3626237952 | bytes 10616832 | tf_op jit(solution)/shard_map/dot_general | solution.py:226
  351.9 47.1 %reduce-scatter.2.cloned.1.call-done = bf16[768,768]{0,1:T(8,128)(2,1)} async-done(((bf16[3072,768]{0,1:T(8,128)(2,1)}), bf16[768,768]{0,1:T(8,128)(2,1)}) %reduce-scatter.2.cloned.1.call-update) | async-done | bytes 1179664 | tf_op jit(solution)/shard_map/reduce_scatter | solution.py:225
  399.0 5.0 %fusion.10 = bf16[1536,768]{1,0:T(8,128)(2,1)} fusion(bf16[768,768]{0,1:T(8,128)(2,1)} %reduce-scatter.2.cloned.1.call-done, s32[1536]{0:T(1024)S(1)} %eq.93, pred[1536]{0:T(1024)(128)(4,1)S(1)} %and.30), kind=kOutput, calls=%fused_computation.18 | convolution fusion | flops 1815478272 | bytes 3546624 | tf_op jit(solution)/shard_map/dot_general | solution.py:239
  404.1 5.5 %all-to-all-start.1 = ((bf16[8,192,768]{2,1,0:T(8,128)(2,1)}), bf16[8,192,768]{2,1,0:T(8,128)(2,1)S(1)}, u32[]{:S(2)}, u32[]{:S(2)}) async-start(bf16[8,192,768]{2,1,0:T(8,128)(2,1)} %bitcast.25), calls=%async_computation.2 | async-start | bytes 4718592 | tf_op jit(solution)/shard_map/all_to_all | solution.py:240
  410.4 2.0 fusion.15
  412.3 51.1 %all-to-all-done.1 = bf16[8,192,768]{2,1,0:T(8,128)(2,1)S(1)} async-done(((bf16[8,192,768]{2,1,0:T(8,128)(2,1)}), bf16[8,192,768]{2,1,0:T(8,128)(2,1)S(1)}, u32[]{:S(2)}, u32[]{:S(2)}) %all-to-all-start.1) | async-done | bytes 2359328 | tf_op jit(solution)/shard_map/all_to_all | solution.py:240
  463.4 3.6 add_convert_fusion
  467.1 1.6 pad_maximum_fusion
  (71 shorter events, 21.2 us)
Async XLA Ops:
  13.7 61.3 %all-to-all-start = ((bf16[8,192,768]{2,1,0:T(8,128)(2,1)}), bf16[8,192,768]{2,1,0:T(8,128)(2,1)S(1)}, u32[]{:S(2)}, u32[]{:S(2)}) async-start(bf16[8,192,768]{2,1,0:T(8,128)(2,1)} %bitcast.26), calls=%async_computation | async-start | bytes 4718592 | tf_op jit(solution)/shard_map/all_to_all | solution.py:207
  21.1 95.2 %all-gather.3.cloned.1.call-start = ((), (), s32[]{:S(2)}) async-start(), calls=%async_computation.4 | async-start | bytes 5898240 | tf_op jit(solution)/shard_map/all_gather | solution.py:222
  75.0 41.4 %copy-start.1 = (f32[3072]{0:T(1024)S(1)}, f32[3072]{0:T(1024)}, u32[]{:S(2)}) copy-start(f32[3072]{0:T(1024)} %param.17) | copy-start | bytes 36868
  75.0 41.4 %copy-start.2 = (f32[128]{0:T(128)S(1)}, f32[128]{0:T(128)}, u32[]{:S(2)}) copy-start(f32[128]{0:T(128)} %param.20) | copy-start | bytes 1540
  75.0 41.4 %copy-start.3 = (f32[128]{0:T(128)S(1)}, f32[128]{0:T(128)}, u32[]{:S(2)}) copy-start(f32[128]{0:T(128)} %param.21) | copy-start | bytes 1540
  79.7 319.3 %reduce-scatter.2.cloned.1.call-start = ((), (), s32[]{:S(2)}) async-start(), calls=%async_computation.3 | async-start | bytes 5898240 | tf_op jit(solution)/shard_map/reduce_scatter | solution.py:225
  137.4 28.8 %collective-permute-start = (bf16[768,768]{1,0:T(8,128)(2,1)S(1)}, bf16[768,768]{1,0:T(8,128)(2,1)S(1)}, u32[]{:S(2)}, u32[]{:S(2)}) collective-permute-start(bf16[768,768]{1,0:T(8,128)(2,1)S(1)} %get-tuple-element.17.refs_1_), channel_id=1, source_target_pairs={{0,8},{8,16},{16,24},{24,28},{28,20},{20,12},{12,4},{4,0},{1,9},{9... | collective-permute-start | bytes 3538952 | tf_op jit(solution)/shard_map/ppermute | solution.py:167
  138.9 28.8 %collective-permute-start.4 = (bf16[768,768]{1,0:T(8,128)(2,1)S(1)}, bf16[768,768]{1,0:T(8,128)(2,1)S(1)}, u32[]{:S(2)}, u32[]{:S(2)}) collective-permute-start(bf16[768,768]{1,0:T(8,128)(2,1)S(1)} %get-tuple-element.18.refs_2_), channel_id=1, source_target_pairs={{8,0},{16,8},{24,16},{28,24},{20,28},{12,20},{4,12},{0,4},{9,1},{1... | collective-permute-start | bytes 3538952 | tf_op jit(solution)/shard_map/ppermute | solution.py:168
  139.4 53.6 %collective-permute-start.8 = (bf16[768,768]{1,0:T(8,128)(2,1)S(1)}, bf16[768,768]{1,0:T(8,128)(2,1)S(1)}, u32[]{:S(2)}, u32[]{:S(2)}) collective-permute-start(bf16[768,768]{1,0:T(8,128)(2,1)S(1)} %get-tuple-element.17.refs_1_), channel_id=1, source_target_pairs={{8,0},{16,8},{24,16},{28,24},{20,28},{12,20},{4,12},{0,4},{9,1},{1... | collective-permute-start | bytes 3538952 | tf_op jit(solution)/shard_map/ppermute | solution.py:168
  140.9 52.7 %collective-permute-start.11 = (bf16[768,768]{1,0:T(8,128)(2,1)S(1)}, bf16[768,768]{1,0:T(8,128)(2,1)S(1)}, u32[]{:S(2)}, u32[]{:S(2)}) collective-permute-start(bf16[768,768]{1,0:T(8,128)(2,1)S(1)} %get-tuple-element.18.refs_2_), channel_id=1, source_target_pairs={{0,8},{8,16},{16,24},{24,28},{28,20},{20,12},{12,4},{4,0},{1,9},{9... | collective-permute-start | bytes 3538952 | tf_op jit(solution)/shard_map/ppermute | solution.py:167
  166.2 50.6 %collective-permute-start.1 = (bf16[768,768]{1,0:T(8,128)(2,1)S(1)}, bf16[768,768]{1,0:T(8,128)(2,1)S(1)}, u32[]{:S(2)}, u32[]{:S(2)}) collective-permute-start(bf16[768,768]{1,0:T(8,128)(2,1)S(1)} %collective-permute-done.refs_1_), channel_id=1, source_target_pairs={{0,8},{8,16},{16,24},{24,28},{28,20},{20,12},{12,4},{4,0},{1,9},{9... | collective-permute-start | bytes 3538952 | tf_op jit(solution)/shard_map/ppermute | solution.py:167
  167.7 65.5 %copy-start.7 = (bf16[768,768]{1,0:T(8,128)(2,1)}, bf16[768,768]{1,0:T(8,128)(2,1)S(1)}, u32[]{:S(2)}) copy-start(bf16[768,768]{1,0:T(8,128)(2,1)S(1)} %collective-permute-done.4.refs_4_) | copy-start | bytes 3538948
  167.7 50.6 %collective-permute-start.5 = (bf16[768,768]{1,0:T(8,128)(2,1)S(1)}, bf16[768,768]{1,0:T(8,128)(2,1)S(1)}, u32[]{:S(2)}, u32[]{:S(2)}) collective-permute-start(bf16[768,768]{1,0:T(8,128)(2,1)S(1)} %collective-permute-done.4.refs_4_), channel_id=1, source_target_pairs={{8,0},{16,8},{24,16},{28,24},{20,28},{12,20},{4,12},{0,4},{9,1},{1... | collective-permute-start | bytes 3538952 | tf_op jit(solution)/shard_map/ppermute | solution.py:168
  193.0 50.6 %collective-permute-start.9 = (bf16[768,768]{1,0:T(8,128)(2,1)S(1)}, bf16[768,768]{1,0:T(8,128)(2,1)S(1)}, u32[]{:S(2)}, u32[]{:S(2)}) collective-permute-start(bf16[768,768]{1,0:T(8,128)(2,1)S(1)} %collective-permute-done.8.refs_2_), channel_id=1, source_target_pairs={{8,0},{16,8},{24,16},{28,24},{20,28},{12,20},{4,12},{0,4},{9,1},{1... | collective-permute-start | bytes 3538952 | tf_op jit(solution)/shard_map/ppermute | solution.py:168
  193.6 50.6 %collective-permute-start.12 = (bf16[768,768]{1,0:T(8,128)(2,1)S(1)}, bf16[768,768]{1,0:T(8,128)(2,1)}, u32[]{:S(2)}, u32[]{:S(2)}) collective-permute-start(bf16[768,768]{1,0:T(8,128)(2,1)S(1)} %collective-permute-done.11.refs_3_), channel_id=1, source_target_pairs={{0,8},{8,16},{16,24},{24,28},{28,20},{20,12},{12,4},{4,0},{1,9},{9... | collective-permute-start | bytes 3538952 | tf_op jit(solution)/shard_map/ppermute | solution.py:167
  216.8 55.0 %collective-permute-start.2 = (bf16[768,768]{1,0:T(8,128)(2,1)S(1)}, bf16[768,768]{1,0:T(8,128)(2,1)S(1)}, u32[]{:S(2)}, u32[]{:S(2)}) collective-permute-start(bf16[768,768]{1,0:T(8,128)(2,1)S(1)} %collective-permute-done.1.refs_1_), channel_id=1, source_target_pairs={{0,8},{8,16},{16,24},{24,28},{28,20},{20,12},{12,4},{4,0},{1,9},{9... | collective-permute-start | bytes 3538952 | tf_op jit(solution)/shard_map/ppermute | solution.py:167
  218.3 55.0 %collective-permute-start.6 = (bf16[768,768]{1,0:T(8,128)(2,1)S(1)}, bf16[768,768]{1,0:T(8,128)(2,1)}, u32[]{:S(2)}, u32[]{:S(2)}) collective-permute-start(bf16[768,768]{1,0:T(8,128)(2,1)S(1)} %collective-permute-done.5.refs_4_), channel_id=1, source_target_pairs={{8,0},{16,8},{24,16},{28,24},{20,28},{12,20},{4,12},{0,4},{9,1},{1... | collective-permute-start | bytes 3538952 | tf_op jit(solution)/shard_map/ppermute | solution.py:168
  243.6 56.6 %collective-permute-start.10 = (bf16[768,768]{1,0:T(8,128)(2,1)S(1)}, bf16[768,768]{1,0:T(8,128)(2,1)S(1)}, u32[]{:S(2)}, u32[]{:S(2)}) collective-permute-start(bf16[768,768]{1,0:T(8,128)(2,1)S(1)} %collective-permute-done.9.refs_2_), channel_id=1, source_target_pairs={{8,0},{16,8},{24,16},{28,24},{20,28},{12,20},{4,12},{0,4},{9,1},{1... | collective-permute-start | bytes 3538952 | tf_op jit(solution)/shard_map/ppermute | solution.py:168
  244.1 56.1 %collective-permute-start.13 = (bf16[768,768]{1,0:T(8,128)(2,1)}, bf16[768,768]{1,0:T(8,128)(2,1)}, u32[]{:S(2)}, u32[]{:S(2)}) collective-permute-start(bf16[768,768]{1,0:T(8,128)(2,1)} %collective-permute-done.12.refs_3_), channel_id=1, source_target_pairs={{0,8},{8,16},{16,24},{24,28},{28,20},{20,12},{12,4},{4,0},{1,9},{9... | collective-permute-start | bytes 3538952 | tf_op jit(solution)/shard_map/ppermute | solution.py:167
  271.8 54.7 %collective-permute-start.3 = (bf16[768,768]{1,0:T(8,128)(2,1)S(1)}, bf16[768,768]{1,0:T(8,128)(2,1)S(1)}, u32[]{:S(2)}, u32[]{:S(2)}) collective-permute-start(bf16[768,768]{1,0:T(8,128)(2,1)S(1)} %collective-permute-done.2.refs_1_), channel_id=1, source_target_pairs={{0,8},{8,16},{16,24},{24,28},{28,20},{20,12},{12,4},{4,0},{1,9},{9... | collective-permute-start | bytes 3538952 | tf_op jit(solution)/shard_map/ppermute | solution.py:167
  273.3 53.1 %collective-permute-start.7 = (bf16[768,768]{1,0:T(8,128)(2,1)}, bf16[768,768]{1,0:T(8,128)(2,1)S(1)}, u32[]{:S(2)}, u32[]{:S(2)}) collective-permute-start(bf16[768,768]{1,0:T(8,128)(2,1)} %collective-permute-done.6.refs_4_), channel_id=1, source_target_pairs={{8,0},{16,8},{24,16},{28,24},{20,28},{12,20},{4,12},{0,4},{9,1},{1... | collective-permute-start | bytes 3538952 | tf_op jit(solution)/shard_map/ppermute | solution.py:168
  273.9 72.4 %slice-start = ((s8[4718592]{0:T(1024)(128)(4,1)}), s8[4194304]{0:T(1024)(128)(4,1)S(1)}, s32[]{:S(2)}) async-start(s8[4718592]{0:T(1024)(128)(4,1)} %bitcast.27), calls=%async_computation.5 | async-start | bytes 8388608
  300.2 46.1 %slice-start.1 = ((s8[4718592]{0:T(1024)(128)(4,1)}), s8[524288]{0:T(1024)(128)(4,1)S(1)}, s32[]{:S(2)}) async-start(s8[4718592]{0:T(1024)(128)(4,1)} %bitcast.27), calls=%async_computation.6 | async-start | bytes 1048576
  404.1 59.4 %all-to-all-start.1 = ((bf16[8,192,768]{2,1,0:T(8,128)(2,1)}), bf16[8,192,768]{2,1,0:T(8,128)(2,1)S(1)}, u32[]{:S(2)}, u32[]{:S(2)}) async-start(bf16[8,192,768]{2,1,0:T(8,128)(2,1)} %bitcast.25), calls=%async_computation.2 | async-start | bytes 4718592 | tf_op jit(solution)/shard_map/all_to_all | solution.py:240
  (6 other events, 114.7 us)
Sparse Core Ops, SparseCore 0:
  79.8 36.4 all-gather.2
  352.1 46.9 reduce-scatter.1

commit v2 on v1

v2 whole, which is shorter than its diff:
```python
import functools
import math

import jax
import jax.numpy as jnp
from jax import lax
from jax.experimental import pallas as pl
from jax.experimental.pallas import tpu as pltpu
from jax.sharding import PartitionSpec as P

HD = 128
eps = 1e-06
VMEM_BYTES = 50 * 1024 * 1024


def qkv_kernel(chunks, group, *refs):
    x_refs = refs[:chunks]
    w_ref, scale_ref, shift_ref, qg_ref, kg_ref, q_ref, k_ref, v_ref, normed_ref = refs[chunks:]
    parts, half, width = x_refs[0].shape
    pieces = [
        (x_refs[c], j, slice((j * chunks + c) * width, (j * chunks + c + 1) * width))
        for j in range(parts)
        for c in range(chunks)
    ]
    features = parts * chunks * width
    tile = 256
    out_tile = half // 2

    @pl.when(pl.program_id(0) == 0)
    def _():
        def rows_step(i, carry):
            rows = pl.ds(pl.multiple_of(i * tile, tile), tile)
            total = jnp.zeros((tile, 1), jnp.float32)
            squares = jnp.zeros((tile, 1), jnp.float32)
            for x_ref, j, cols in pieces:
                x = x_ref[j, rows, :].astype(jnp.float32)
                total += jnp.sum(x, axis=1, keepdims=True)
                squares += jnp.sum(x * x, axis=1, keepdims=True)
            mean = total / features
            inv = lax.rsqrt(squares / features - mean * mean + eps)
            for x_ref, j, cols in pieces:
                x = x_ref[j, rows, :].astype(jnp.float32)
                normed_ref[rows, cols] = (
                    (x - mean) * inv * (1.0 + scale_ref[:, cols]) + shift_ref[:, cols]
                ).astype(jnp.bfloat16)
            return carry

        lax.fori_loop(0, half // tile, rows_step, 0)

    def norm(values, gain):
        return values * lax.rsqrt(jnp.mean(values * values, axis=-1, keepdims=True) + eps) * gain

    def out_step(i, carry):
        rows = pl.ds(pl.multiple_of(i * out_tile, out_tile), out_tile)
        out = jnp.dot(normed_ref[rows, :], w_ref[...], preferred_element_type=jnp.float32)
        for g in range(group):
            base = g * 3 * HD
            cols = slice(g * HD, (g + 1) * HD)
            q_ref[rows, cols] = norm(out[:, base : base + HD], qg_ref[...]).astype(jnp.bfloat16)
            k_ref[rows, cols] = norm(out[:, base + HD : base + 2 * HD], kg_ref[...]).astype(jnp.bfloat16)
            v_ref[rows, cols] = out[:, base + 2 * HD : base + 3 * HD].astype(jnp.bfloat16)
        return carry

    lax.fori_loop(0, half // out_tile, out_step, 0)


def project_qkv(gathered, w_qkv, scale, shift, q_gain, k_gain):
    parts, half, width = gathered[0].shape
    depth, cols = w_qkv.shape
    heads = cols // (3 * HD)
    group = 2 if heads % 2 == 0 else 1
    whole = lambda shape: pl.BlockSpec(shape, lambda i: (0,) * len(shape))
    out = jax.ShapeDtypeStruct((half, heads * HD), jnp.bfloat16)
    return pl.pallas_call(
        functools.partial(qkv_kernel, len(gathered), group),
        grid=(heads // group,),
        in_specs=[whole((parts, half, width))] * len(gathered)
        + [
            pl.BlockSpec((depth, group * 3 * HD), lambda i: (0, i)),
            whole((1, depth)),
            whole((1, depth)),
            whole((1, HD)),
            whole((1, HD)),
        ],
        out_specs=[pl.BlockSpec((half, group * HD), lambda i: (0, i))] * 3,
        out_shape=[out] * 3,
        scratch_shapes=[pltpu.VMEM((half, depth), jnp.bfloat16)],
        compiler_params=pltpu.CompilerParams(
            dimension_semantics=("arbitrary",), vmem_limit_bytes=VMEM_BYTES
        ),
        cost_estimate=pl.CostEstimate(
            flops=2 * half * depth * cols, bytes_accessed=2 * depth * cols + 8 * half * depth, transcendentals=0
        ),
    )(*gathered, w_qkv, scale[None, :], shift[None, :], q_gain[None, :], k_gain[None, :])


def flash_kernel(blocks, group, first, last, *refs):
    q_ref = refs[0]
    k_refs = refs[1 : 1 + blocks]
    v_refs = refs[1 + blocks : 1 + 2 * blocks]
    rest = refs[1 + 2 * blocks :]
    factor = HD ** (-0.5) * math.log2(math.e)
    if not first:
        old_top, old_total = rest[:2]
        rest = rest[2:]
    for g in range(group):
        cols = slice(g * HD, (g + 1) * HD)
        wide = slice(2 * g * HD, 2 * (g + 1) * HD)
        q = q_ref[:, cols]
        scores = [
            lax.dot_general(q, k[:, cols], (((1,), (1,)), ((), ())), preferred_element_type=jnp.float32)
            for k in k_refs
        ]
        top = functools.reduce(jnp.maximum, [jnp.max(s, axis=1, keepdims=True) for s in scores])
        if not first:
            old = old_top[:, g * HD : g * HD + 1]
            top = jnp.maximum(top, old)
        total = None
        for s, v in zip(scores, v_refs):
            probs = jnp.exp2((s - top) * factor).astype(jnp.bfloat16)
            value = v[:, cols]
            values = jnp.concatenate([value, jnp.ones_like(value)], axis=1)
            term = jnp.dot(probs, values, preferred_element_type=jnp.float32)
            total = term if total is None else total + term
        if not first:
            total = total + old_total[:, wide] * jnp.exp2((old - top) * factor)
        if last:
            rest[0][:, cols] = (total[:, :HD] / total[:, HD:]).astype(jnp.bfloat16)
        else:
            rest[0][:, cols] = jnp.broadcast_to(top, (top.shape[0], HD))
            rest[1][:, wide] = total


def flash(query, keys, values, state, last):
    rows, width = query.shape
    heads = width // HD
    group = 2 if heads % 2 == 0 else 1
    blocks = len(keys)
    count = keys[0].shape[0]
    tile = 256
    first = state is None
    row_spec = pl.BlockSpec((tile, group * HD), lambda h, i: (i, h))
    acc_spec = pl.BlockSpec((tile, 2 * group * HD), lambda h, i: (i, h))
    key_spec = pl.BlockSpec((count, group * HD), lambda h, i: (0, h))
    state_specs = [row_spec, acc_spec]
    state_shapes = [
        jax.ShapeDtypeStruct((rows, width), jnp.float32),
        jax.ShapeDtypeStruct((rows, 2 * width), jnp.float32),
    ]
    state = () if first else tuple(state)
    return pl.pallas_call(
        functools.partial(flash_kernel, blocks, group, first, last),
        grid=(heads // group, rows // tile),
        in_specs=[row_spec] + [key_spec] * (2 * blocks) + ([] if first else state_specs),
        out_specs=row_spec if last else state_specs,
        out_shape=jax.ShapeDtypeStruct((rows, width), jnp.bfloat16) if last else state_shapes,
        compiler_params=pltpu.CompilerParams(
            dimension_semantics=("arbitrary", "arbitrary"), vmem_limit_bytes=VMEM_BYTES
        ),
        cost_estimate=pl.CostEstimate(
            flops=8 * rows * count * blocks * width,
            bytes_accessed=4 * count * blocks * width + 16 * rows * width,
            transcendentals=rows * count * blocks * heads,
        ),
    )(query, *keys, *values, *state)


def ring_pairs(shards):
    depth = 4 if shards % 8 == 0 else 1
    across = shards // depth
    order = []
    for y in range(across):
        line = range(depth) if y % 2 == 0 else range(depth - 1, -1, -1)
        order += [z * across + y for z in line]
    right = [(order[i], order[(i + 1) % shards]) for i in range(shards)]
    return right, [(b, a) for a, b in right]


def attend(query, keys, values):
    shards = lax.axis_size("seq")
    right, left = ring_pairs(shards)
    move_right = lambda x: lax.ppermute(x, "seq", right)
    move_left = lambda x: lax.ppermute(x, "seq", left)
    fk, fv, bk, bv = keys, values, keys, values
    state = None
    here_k, here_v = [keys], [values]

    def after(x):
        return x if state is None else lax.optimization_barrier((x, state[0]))[0]

    for step in range(1, shards // 2):
        fk, bk, fv, bv = (
            move_right(after(fk)),
            move_left(after(bk)),
            move_right(after(fv)),
            move_left(after(bv)),
        )
        state = flash(query, here_k, here_v, state, False)
        here_k, here_v = [fk, bk], [fv, bv]
    fk, bv = move_right(after(fk)), move_left(after(bv))
    state = flash(query, here_k, here_v, state, False)
    return flash(query, [fk], [bv], state, True)


def body(
    tokens, w_qkv, w_out, dest_shard, dest_index, merge_weight, shift, scale, gate, q_gain, k_gain
):
    shards = lax.axis_size("seq")
    mine = lax.axis_index("seq")
    feature_part = lax.axis_index("head")
    rows, width = tokens.shape
    half = rows // 2
    capacity = max(2, 2 * half // shards)
    slots_all = shards * capacity
    owner = dest_shard[:, 0].reshape(shards, half)
    index = dest_index.reshape(shards, half)
    weight = merge_weight.astype(jnp.float32).reshape(shards, half)
    my_owner = lax.dynamic_index_in_dim(owner, mine, 0, keepdims=False)
    hot = jnp.concatenate(
        [my_owner[None, :] == jnp.arange(shards)[:, None], owner == mine], axis=0
    ).astype(jnp.bfloat16)
    upper = (jnp.arange(half)[:, None] <= jnp.arange(half)[None, :]).astype(jnp.bfloat16)
    place = jnp.dot(hot, upper, preferred_element_type=jnp.float32).astype(jnp.int32) - 1
    my_rank = jnp.sum(jnp.where(hot[:shards] > 0, place[:shards], 0), axis=0)
    my_slot = my_owner * capacity + my_rank
    rank = place[shards:]
    packer = (jnp.arange(slots_all)[:, None] == my_slot[None, :]).astype(jnp.bfloat16)
    parts = lax.axis_size("head")
    chunks = max(1, width // 384)
    piece = width // chunks
    kept = tokens[:half]
    moved = tokens[half:]

    def exchange(x):
        return lax.all_to_all(
            x.reshape(shards, capacity, piece), "seq", split_axis=0, concat_axis=0, tiled=True
        ).reshape(slots_all, piece)

    incoming = []
    for c in range(chunks):
        outgoing = jnp.dot(
            packer, moved[:, c * piece : (c + 1) * piece], preferred_element_type=jnp.float32
        ).astype(jnp.bfloat16)
        incoming.append(exchange(outgoing))
    chosen = (owner == mine)[:, :, None] & (rank[:, :, None] == jnp.arange(capacity)[None, None, :])
    slot_weight = jnp.sum(jnp.where(chosen, weight[:, :, None], 0.0), axis=1).reshape(slots_all)
    slot_index = jnp.sum(jnp.where(chosen, index[:, :, None], 0), axis=1).reshape(slots_all)
    slot_used = jnp.any(chosen, axis=1).reshape(slots_all)
    target_hot = (jnp.arange(half)[:, None] == slot_index[None, :]) & slot_used[None, :]
    spread = jnp.where(target_hot, slot_weight[None, :], 0.0)
    spread_b = spread.astype(jnp.bfloat16)
    denom = 1.0 + jnp.sum(spread, axis=1, keepdims=True)
    gathered = []
    for c in range(chunks):
        numer = kept[:, c * piece : (c + 1) * piece].astype(jnp.float32) + jnp.dot(
            spread_b, incoming[c], preferred_element_type=jnp.float32
        )
        merged = (numer / denom).astype(jnp.bfloat16)
        gathered.append(lax.all_gather(merged, "head", axis=0, tiled=False))
    query, keys, values = project_qkv(gathered, w_qkv, scale, shift, q_gain, k_gain)
    attended = attend(query, keys, values)
    gate_here = lax.dynamic_slice_in_dim(gate, feature_part * width, width)
    picker = ((jnp.arange(half)[None, :] == slot_index[:, None]) & slot_used[:, None]).astype(
        jnp.bfloat16
    )
    w_parts = w_out.reshape(w_out.shape[0], parts, chunks, piece)
    shares = [
        lax.psum_scatter(
            lax.dot_general(
                w_parts[:, :, c].reshape(w_out.shape[0], parts * piece),
                attended,
                (((0,), (1,)), ((), ())),
                preferred_element_type=jnp.float32,
            ).astype(jnp.bfloat16),
            "head",
            scatter_dimension=0,
            tiled=True,
        )
        for c in range(chunks)
    ]
    kept_out, moved_out = [], []
    for c in range(chunks):
        cols = slice(c * piece, (c + 1) * piece)
        proj = shares[c].T
        returning = jnp.dot(picker, proj, preferred_element_type=jnp.float32).astype(jnp.bfloat16)
        back = exchange(returning)
        kept_out.append(kept[:, cols].astype(jnp.float32) + gate_here[cols] * proj.astype(jnp.float32))
        moved_proj = lax.dot_general(
            packer, back, (((0,), (0,)), ((), ())), preferred_element_type=jnp.float32
        )
        moved_out.append(moved[:, cols].astype(jnp.float32) + gate_here[cols] * moved_proj)
    return jnp.concatenate(
        [
            jnp.concatenate(kept_out, axis=1).astype(jnp.bfloat16),
            jnp.concatenate(moved_out, axis=1).astype(jnp.bfloat16),
        ],
        axis=0,
    )


def solution(mesh):
    placed = (
        P("seq", "head"),
        P(None, "head"),
        P("head", None),
        P(),
        P(),
        P(),
        P(),
        P(),
        P(),
        P(),
        P(),
    )
    return jax.shard_map(
        body, mesh=mesh, in_specs=placed, out_specs=P("seq", "head"), check_vma=False
    )
```

time: 476 us -> 448 us (0.941)
  waiting for transfers between devices: 266 us -> 205 us
  Pallas kernels: 133 us -> 96.5 us
  blocking collectives: 0 us -> 32.5 us
  local copies, waits for them, and re-layouts: 2.64 us -> 22.7 us
  starting transfers between devices: 27.3 us -> 33.2 us
  matrix products: 24 us -> 29.3 us
  other arithmetic: 8.9 us -> 13.9 us
    all_to_all x2 -> x3, waiting for transfers between devices: 101 us -> 38.1 us  [exchange(): lax.all_to_all(x.reshape(shards, capacity, piece), 'seq', split_axis=0, c...]
    unnamed x2 -> x6, waiting for transfers between devices: 0.03 us -> 52.3 us
    reduce_scatter x1 -> x0, waiting for transfers between devices: 47.1 us -> none  [body(): lax.psum_scatter(lax.dot_general(w_out, attended, (((0,), (1,)), ((), ())...]
    pallas_call x6, Pallas kernels: 133 us -> 96.5 us  [the longest x5 75.8 us: flash(): pl.pallas_call(functools.partial(flash_kernel, blocks, group, first, last...]
    all_to_all x0 -> x1, blocking collectives: none -> 32.5 us  [exchange(): lax.all_to_all(x.reshape(shards, capacity, piece), 'seq', split_axis=0, c...]
    ppermute x7, waiting for transfers between devices: 35.2 us -> 64.7 us  [attend(): move_left = lambda x: lax.ppermute(x, 'seq', left)]
    ppermute x7, waiting for transfers between devices: 46.5 us -> 27.5 us  [attend(): move_right = lambda x: lax.ppermute(x, 'seq', right)]
    all_gather x1 -> x2, waiting for transfers between devices: 36.6 us -> 22.7 us  [body(): gathered.append(lax.all_gather(merged, 'head', axis=0, tiled=False))]
  transfers between devices with their start and end apart: 18 -> 21, of which waited for: 8 -> 14; matrix products, arithmetic and copies ran while one was open for 1% -> 11% of each run, Pallas kernels for 20% -> 14%
where the time goes in v2:
time: 448 us; the launch traced here: 447 us
  waiting for transfers between devices  205 us (46%)
  Pallas kernels  96.5 us (22%)
  starting transfers between devices  33.2 us (7%)
  blocking collectives  32.5 us (7%)
  matrix products  29.3 us (7%)
  local copies, waits for them, and re-layouts  22.7 us (5%)
  other arithmetic  13.9 us (3%)
  between operations  13.4 us (3%)
    pallas_call x5, Pallas kernels, flash(): pl.pallas_call(functools.partial(flash_kernel, blocks, group, first, last...  75.8 us
    ppermute x7, waiting for transfers between devices, attend(): move_left = lambda x: lax.ppermute(x, 'seq', left)  64.7 us
    unnamed x6, waiting for transfers between devices  52.3 us
    all_to_all x3, waiting for transfers between devices, exchange(): lax.all_to_all(x.reshape(shards, capacity, piece), 'seq', split_axis=0, c...  38.1 us
    all_to_all x1, blocking collectives, exchange(): lax.all_to_all(x.reshape(shards, capacity, piece), 'seq', split_axis=0, c...  32.5 us
    ppermute x7, waiting for transfers between devices, attend(): move_right = lambda x: lax.ppermute(x, 'seq', right)  27.5 us
    all_gather x2, waiting for transfers between devices, body(): gathered.append(lax.all_gather(merged, 'head', axis=0, tiled=False))  22.7 us
    pallas_call x1, Pallas kernels, project_qkv(): pl.pallas_call(functools.partial(qkv_kernel, len(gathered), group), grid=...  20.7 us
  transfers between devices with their start and end apart: 21, of which 14 were waited for; matrix products, arithmetic and copies ran while one was open for 11% of the time, Pallas kernels for 14%

profile of v2, /device:TPU:0, one launch (start us, length us, event | category | flops | bytes accessed | tf_op | source)
XLA Modules:
  0.0 446.9 jit_solution(14269671633641436758)
XLA Ops:
  12.9 7.4 %all-to-all-start = ((bf16[8,192,384]{2,1,0:T(8,128)(2,1)}), bf16[8,192,384]{2,1,0:T(8,128)(2,1)S(1)}, u32[]{:S(2)}, u32[]{:S(2)}) async-start(bf16[8,192,384]{2,1,0:T(8,128)(2,1)} %bitcast), calls=%async_computation | async-start | bytes 2359296 | tf_op jit(solution)/shard_map/all_to_all | solution.py:235
  33.9 15.0 %all-to-all-done = bf16[8,192,384]{2,1,0:T(8,128)(2,1)S(1)} async-done(((bf16[8,192,384]{2,1,0:T(8,128)(2,1)}), bf16[8,192,384]{2,1,0:T(8,128)(2,1)S(1)}, u32[]{:S(2)}, u32[]{:S(2)}) %all-to-all-start) | async-done | bytes 1179680 | tf_op jit(solution)/shard_map/all_to_all | solution.py:235
  53.4 32.5 %all_to_all.20 = bf16[8,192,384]{2,1,0:T(8,128)(2,1)S(1)} all-to-all(bf16[8,192,384]{2,1,0:T(8,128)(2,1)S(1)} %bitcast.48), channel_id=1, replica_groups=mesh['seq'=8,'head'=4] {'seq'}, dimensions={0} | all-to-all | bytes 2359296 | tf_op jit(solution)/shard_map/all_to_all | solution.py:235
  88.5 22.6 %all-gather.7.cloned.1.call-done = bf16[3072,384]{1,0:T(8,128)(2,1)} async-done(((bf16[768,384]{1,0:T(8,128)(2,1)}), bf16[3072,384]{1,0:T(8,128)(2,1)}) %all-gather.7.cloned.1.call-update) | async-done | bytes 2359312 | tf_op jit(solution)/shard_map/all_gather | solution.py:259
  111.2 20.7 %shard_map.109 = (bf16[768,768]{1,0:T(8,128)(2,1)S(1)}, bf16[768,768]{1,0:T(8,128)(2,1)S(1)}, bf16[768,768]{1,0:T(8,128)(2,1)S(1)}) custom-call(bf16[4,768,384]{2,1,0:T(8,128)(2,1)} %bitcast.49, bf16[4,768,384]{2,1,0:T(8,128)(2,1)} %bitcast.50, bf16[3072,2304]{1,0:T(8,128)(2,1)} %refs_2_.1, f32[1,3072]{1,0:T(1,128)S(1)} %bitcast.38, f32[1,3072]{1,0:T(1,128)S(1)} %bitcast.39, ...), custom_call_target="tpu_custom_call" | custom-call | flops 10871635968 | bytes 33030144 | tf_op jit(solution)/shard_map/pallas_call | solution.py:74
  136.0 9.5 %shard_map.110 = (f32[768,768]{1,0:T(8,128)}, f32[768,1536]{1,0:T(8,128)}) custom-call(bf16[768,768]{1,0:T(8,128)(2,1)S(1)} %get-tuple-element.26.refs_0_, bf16[768,768]{1,0:T(8,128)(2,1)S(1)} %get-tuple-element.27.refs_1_, bf16[768,768]{1,0:T(8,128)(2,1)S(1)} %get-tuple-element.28.refs_2_), custom_call_target="tpu_custom_call" | custom-call | flops 3623878656 | bytes 11796480 | tf_op jit(solution)/shard_map/pallas_call | solution.py:151
  145.6 15.2 %collective-permute-done.refs_1_ = bf16[768,768]{1,0:T(8,128)(2,1)S(1)} collective-permute-done((bf16[768,768]{1,0:T(8,128)(2,1)S(1)}, bf16[768,768]{1,0:T(8,128)(2,1)S(1)}, u32[]{:S(2)}, u32[]{:S(2)}) %collective-permute-start) | collective-permute-done | bytes 1179680 | tf_op jit(solution)/shard_map/ppermute | solution.py:182
  162.9 24.7 %collective-permute-done.2.refs_2_ = bf16[768,768]{1,0:T(8,128)(2,1)S(1)} collective-permute-done((bf16[768,768]{1,0:T(8,128)(2,1)S(1)}, bf16[768,768]{1,0:T(8,128)(2,1)S(1)}, u32[]{:S(2)}, u32[]{:S(2)}) %collective-permute-start.2) | collective-permute-done | bytes 1179680 | tf_op jit(solution)/shard_map/ppermute | solution.py:183
  189.6 18.1 %shard_map.111 = (f32[768,768]{1,0:T(8,128)}, f32[768,1536]{1,0:T(8,128)}) custom-call(bf16[768,768]{1,0:T(8,128)(2,1)S(1)} %get-tuple-element.26.refs_0_, bf16[768,768]{1,0:T(8,128)(2,1)S(1)} %collective-permute-done.refs_1_, bf16[768,768]{1,0:T(8,128)(2,1)S(1)} %collective-permute-done.2.refs_2_, bf16[768,768]{1,0:T(8,128)(2,1)} %copy-done.18, ...), custom_call_target="tpu_custom_call" | custom-call | flops 7247757312 | bytes 14155776 | tf_op jit(solution)/shard_map/pallas_call | solution.py:151
  213.4 24.7 %collective-permute-done.6.refs_2_ = bf16[768,768]{1,0:T(8,128)(2,1)S(1)} collective-permute-done((bf16[768,768]{1,0:T(8,128)(2,1)S(1)}, bf16[768,768]{1,0:T(8,128)(2,1)S(1)}, u32[]{:S(2)}, u32[]{:S(2)}) %collective-permute-start.6) | collective-permute-done | bytes 1179680 | tf_op jit(solution)/shard_map/ppermute | solution.py:183
  240.2 18.1 %shard_map.112 = (f32[768,768]{1,0:T(8,128)}, f32[768,1536]{1,0:T(8,128)}) custom-call(bf16[768,768]{1,0:T(8,128)(2,1)S(1)} %get-tuple-element.26.refs_0_, bf16[768,768]{1,0:T(8,128)(2,1)S(1)} %collective-permute-done.1.refs_1_, bf16[768,768]{1,0:T(8,128)(2,1)S(1)} %collective-permute-done.6.refs_2_, bf16[768,768]{1,0:T(8,128)(2,1)} %collective-permute-done.7.refs_3_, ...), custom_call_target="tpu_custom_call" | custom-call | flops 7247757312 | bytes 14155776 | tf_op jit(solution)/shard_map/pallas_call | solution.py:151
  264.1 6.6 %copy.22 = bf16[768,3072]{0,1:T(8,128)(2,1)} copy(bf16[768,3072]{1,0:T(8,128)(2,1)} %param.13) | data formatting | bytes 9437184 | tf_op args[2]
  270.7 4.2 fusion.60
  274.9 13.8 %collective-permute-done.12.refs_2_ = bf16[768,768]{1,0:T(8,128)(2,1)S(1)} collective-permute-done((bf16[768,768]{1,0:T(8,128)(2,1)S(1)}, bf16[768,768]{1,0:T(8,128)(2,1)S(1)}, u32[]{:S(2)}, u32[]{:S(2)}) %collective-permute-start.12) | collective-permute-done | bytes 1179680 | tf_op jit(solution)/shard_map/ppermute | solution.py:183
  288.7 18.1 %shard_map.113 = (f32[768,768]{1,0:T(8,128)}, f32[768,1536]{1,0:T(8,128)}) custom-call(bf16[768,768]{1,0:T(8,128)(2,1)S(1)} %copy-done.5, bf16[768,768]{1,0:T(8,128)(2,1)S(1)} %collective-permute-done.5.refs_1_, bf16[768,768]{1,0:T(8,128)(2,1)S(1)} %collective-permute-done.12.refs_2_, bf16[768,768]{1,0:T(8,128)(2,1)} %collective-permute-done.13.refs_3_, ...), custom_call_target="tpu_custom_call" | custom-call | flops 7247757312 | bytes 14155776 | tf_op jit(solution)/shard_map/pallas_call | solution.py:151
  306.8 5.1 %collective-permute-done.9.refs_1_ = bf16[768,768]{1,0:T(8,128)(2,1)} collective-permute-done((bf16[768,768]{1,0:T(8,128)(2,1)S(1)}, bf16[768,768]{1,0:T(8,128)(2,1)}, u32[]{:S(2)}, u32[]{:S(2)}) %collective-permute-start.9) | collective-permute-done | bytes 1179680 | tf_op jit(solution)/shard_map/ppermute | solution.py:182
  313.1 12.0 %shard_map.114 = bf16[768,768]{1,0:T(8,128)(2,1)S(1)} custom-call(bf16[768,768]{1,0:T(8,128)(2,1)S(1)} %copy-done.5, bf16[768,768]{1,0:T(8,128)(2,1)} %collective-permute-done.9.refs_1_, bf16[768,768]{1,0:T(8,128)(2,1)} %collective-permute-done.11.refs_2_, f32[768,768]{1,0:T(8,128)} %get-tuple-element.45.refs_3_, f32[768,1536]{1,0:T(8,128)} %get-tuple-element.46.refs_4_), custom_call_target="tpu_custom_call" | custom-call | flops 3623878656 | bytes 11796480 | tf_op jit(solution)/shard_map/pallas_call | solution.py:151
  335.8 26.0 %reduce-scatter.9.cloned.1.call-done = bf16[384,768]{1,0:T(8,128)(2,1)} async-done(((bf16[1536,768]{1,0:T(8,128)(2,1)}), bf16[384,768]{1,0:T(8,128)(2,1)}) %reduce-scatter.9.cloned.1.call-update) | async-done | bytes 589840
  361.9 4.0 fusion.17
  365.8 5.5 %all-to-all-start.3 = ((bf16[8,192,384]{2,1,0:T(8,128)(2,1)}), bf16[8,192,384]{2,1,0:T(8,128)(2,1)S(1)}, u32[]{:S(2)}, u32[]{:S(2)}) async-start(bf16[8,192,384]{2,1,0:T(8,128)(2,1)} %bitcast.19), calls=%async_computation.3 | async-start | bytes 2359296 | tf_op jit(solution)/shard_map/all_to_all | solution.py:235
  371.4 26.2 %reduce-scatter.7.cloned.1.call-done = bf16[384,768]{1,0:T(8,128)(2,1)} async-done(((bf16[1536,768]{1,0:T(8,128)(2,1)}), bf16[384,768]{1,0:T(8,128)(2,1)}) %reduce-scatter.7.cloned.1.call-update) | async-done | bytes 589840
  397.5 4.0 fusion.14
  401.5 5.7 %all-to-all-start.2 = ((bf16[8,192,384]{2,1,0:T(8,128)(2,1)}), bf16[8,192,384]{2,1,0:T(8,128)(2,1)}, u32[]{:S(2)}, u32[]{:S(2)}) async-start(bf16[8,192,384]{2,1,0:T(8,128)(2,1)} %bitcast.17), calls=%async_computation.2 | async-start | bytes 2359296 | tf_op jit(solution)/shard_map/all_to_all | solution.py:235
  412.8 23.1 %all-to-all-done.2 = bf16[8,192,384]{2,1,0:T(8,128)(2,1)} async-done(((bf16[8,192,384]{2,1,0:T(8,128)(2,1)}), bf16[8,192,384]{2,1,0:T(8,128)(2,1)}, u32[]{:S(2)}, u32[]{:S(2)}) %all-to-all-start.2) | async-done | bytes 1179680 | tf_op jit(solution)/shard_map/all_to_all | solution.py:235
  (107 shorter events, 70.5 us)
Async XLA Ops:
  12.9 36.0 %copy-start.8 = (bf16[1536,768]{1,0:T(8,128)(2,1)S(1)}, bf16[1536,768]{1,0:T(8,128)(2,1)}, u32[]{:S(2)}) copy-start(bf16[1536,768]{1,0:T(8,128)(2,1)} %param.11) | copy-start | bytes 7077892
  12.9 36.0 %all-to-all-start = ((bf16[8,192,384]{2,1,0:T(8,128)(2,1)}), bf16[8,192,384]{2,1,0:T(8,128)(2,1)S(1)}, u32[]{:S(2)}, u32[]{:S(2)}) async-start(bf16[8,192,384]{2,1,0:T(8,128)(2,1)} %bitcast), calls=%async_computation | async-start | bytes 2359296 | tf_op jit(solution)/shard_map/all_to_all | solution.py:235
  20.3 68.2 %all-gather.5.cloned.1.call-start = ((), (), s32[]{:S(2)}) async-start(), calls=%async_computation.6 | async-start | bytes 2949120 | tf_op jit(solution)/shard_map/all_gather | solution.py:259
  51.9 59.3 %all-gather.7.cloned.1.call-start = ((), (), s32[]{:S(2)}) async-start(), calls=%async_computation.7 | async-start | bytes 2949120 | tf_op jit(solution)/shard_map/all_gather | solution.py:259
  53.4 32.6 %copy-start.9 = (f32[1536]{0:T(1024)S(1)}, f32[1536]{0:T(1024)}, u32[]{:S(2)}) copy-start(f32[1536]{0:T(1024)} %broadcast_in_dim.84) | copy-start | bytes 18436
  88.3 273.6 %reduce-scatter.9.cloned.1.call-start = ((), (), s32[]{:S(2)}) async-start(), calls=%async_computation.9 | async-start | bytes 2949120
  131.9 108.3 %copy-start.4 = (bf16[768,768]{1,0:T(8,128)(2,1)}, bf16[768,768]{1,0:T(8,128)(2,1)S(1)}, u32[]{:S(2)}) copy-start(bf16[768,768]{1,0:T(8,128)(2,1)S(1)} %get-tuple-element.26.refs_0_) | copy-start | bytes 3538948
  131.9 28.9 %collective-permute-start = (bf16[768,768]{1,0:T(8,128)(2,1)S(1)}, bf16[768,768]{1,0:T(8,128)(2,1)S(1)}, u32[]{:S(2)}, u32[]{:S(2)}) collective-permute-start(bf16[768,768]{1,0:T(8,128)(2,1)S(1)} %get-tuple-element.27.refs_1_), channel_id=1, source_target_pairs={{0,8},{8,16},{16,24},{24,28},{28,20},{20,12},{12,4},{4,0},{1,9},{9... | collective-permute-start | bytes 3538952 | tf_op jit(solution)/shard_map/ppermute | solution.py:182
  133.5 28.8 %collective-permute-start.4 = (bf16[768,768]{1,0:T(8,128)(2,1)S(1)}, bf16[768,768]{1,0:T(8,128)(2,1)S(1)}, u32[]{:S(2)}, u32[]{:S(2)}) collective-permute-start(bf16[768,768]{1,0:T(8,128)(2,1)S(1)} %get-tuple-element.28.refs_2_), channel_id=1, source_target_pairs={{8,0},{16,8},{24,16},{28,24},{20,28},{12,20},{4,12},{0,4},{9,1},{1... | collective-permute-start | bytes 3538952 | tf_op jit(solution)/shard_map/ppermute | solution.py:183
  134.0 53.6 %collective-permute-start.2 = (bf16[768,768]{1,0:T(8,128)(2,1)S(1)}, bf16[768,768]{1,0:T(8,128)(2,1)S(1)}, u32[]{:S(2)}, u32[]{:S(2)}) collective-permute-start(bf16[768,768]{1,0:T(8,128)(2,1)S(1)} %get-tuple-element.27.refs_1_), channel_id=1, source_target_pairs={{8,0},{16,8},{24,16},{28,24},{20,28},{12,20},{4,12},{0,4},{9,1},{1... | collective-permute-start | bytes 3538952 | tf_op jit(solution)/shard_map/ppermute | solution.py:183
  135.5 52.6 %collective-permute-start.3 = (bf16[768,768]{1,0:T(8,128)(2,1)S(1)}, bf16[768,768]{1,0:T(8,128)(2,1)S(1)}, u32[]{:S(2)}, u32[]{:S(2)}) collective-permute-start(bf16[768,768]{1,0:T(8,128)(2,1)S(1)} %get-tuple-element.28.refs_2_), channel_id=1, source_target_pairs={{0,8},{8,16},{16,24},{24,28},{28,20},{20,12},{12,4},{4,0},{1,9},{9... | collective-permute-start | bytes 3538952 | tf_op jit(solution)/shard_map/ppermute | solution.py:182
  160.8 50.6 %collective-permute-start.1 = (bf16[768,768]{1,0:T(8,128)(2,1)S(1)}, bf16[768,768]{1,0:T(8,128)(2,1)S(1)}, u32[]{:S(2)}, u32[]{:S(2)}) collective-permute-start(bf16[768,768]{1,0:T(8,128)(2,1)S(1)} %collective-permute-done.refs_1_), channel_id=1, source_target_pairs={{0,8},{8,16},{16,24},{24,28},{28,20},{20,12},{12,4},{4,0},{1,9},{9... | collective-permute-start | bytes 3538952 | tf_op jit(solution)/shard_map/ppermute | solution.py:182
  162.3 50.6 %collective-permute-start.8 = (bf16[768,768]{1,0:T(8,128)(2,1)S(1)}, bf16[768,768]{1,0:T(8,128)(2,1)S(1)}, u32[]{:S(2)}, u32[]{:S(2)}) collective-permute-start(bf16[768,768]{1,0:T(8,128)(2,1)S(1)} %collective-permute-done.4.refs_4_), channel_id=1, source_target_pairs={{8,0},{16,8},{24,16},{28,24},{20,28},{12,20},{4,12},{0,4},{9,1},{1... | collective-permute-start | bytes 3538952 | tf_op jit(solution)/shard_map/ppermute | solution.py:183
  187.6 50.6 %collective-permute-start.6 = (bf16[768,768]{1,0:T(8,128)(2,1)S(1)}, bf16[768,768]{1,0:T(8,128)(2,1)S(1)}, u32[]{:S(2)}, u32[]{:S(2)}) collective-permute-start(bf16[768,768]{1,0:T(8,128)(2,1)S(1)} %collective-permute-done.2.refs_2_), channel_id=1, source_target_pairs={{8,0},{16,8},{24,16},{28,24},{20,28},{12,20},{4,12},{0,4},{9,1},{1... | collective-permute-start | bytes 3538952 | tf_op jit(solution)/shard_map/ppermute | solution.py:183
  188.1 50.6 %collective-permute-start.7 = (bf16[768,768]{1,0:T(8,128)(2,1)S(1)}, bf16[768,768]{1,0:T(8,128)(2,1)}, u32[]{:S(2)}, u32[]{:S(2)}) collective-permute-start(bf16[768,768]{1,0:T(8,128)(2,1)S(1)} %collective-permute-done.3.refs_3_), channel_id=1, source_target_pairs={{0,8},{8,16},{16,24},{24,28},{28,20},{20,12},{12,4},{4,0},{1,9},{9... | collective-permute-start | bytes 3538952 | tf_op jit(solution)/shard_map/ppermute | solution.py:182
  211.3 50.6 %collective-permute-start.5 = (bf16[768,768]{1,0:T(8,128)(2,1)S(1)}, bf16[768,768]{1,0:T(8,128)(2,1)S(1)}, u32[]{:S(2)}, u32[]{:S(2)}) collective-permute-start(bf16[768,768]{1,0:T(8,128)(2,1)S(1)} %collective-permute-done.1.refs_1_), channel_id=1, source_target_pairs={{0,8},{8,16},{16,24},{24,28},{28,20},{20,12},{12,4},{4,0},{1,9},{9... | collective-permute-start | bytes 3538952 | tf_op jit(solution)/shard_map/ppermute | solution.py:182
  212.9 50.7 %collective-permute-start.10 = (bf16[768,768]{1,0:T(8,128)(2,1)S(1)}, bf16[768,768]{1,0:T(8,128)(2,1)}, u32[]{:S(2)}, u32[]{:S(2)}) collective-permute-start(bf16[768,768]{1,0:T(8,128)(2,1)S(1)} %collective-permute-done.8.refs_4_), channel_id=1, source_target_pairs={{8,0},{16,8},{24,16},{28,24},{20,28},{12,20},{4,12},{0,4},{9,1},{1... | collective-permute-start | bytes 3538952 | tf_op jit(solution)/shard_map/ppermute | solution.py:183
  238.1 50.6 %collective-permute-start.12 = (bf16[768,768]{1,0:T(8,128)(2,1)S(1)}, bf16[768,768]{1,0:T(8,128)(2,1)S(1)}, u32[]{:S(2)}, u32[]{:S(2)}) collective-permute-start(bf16[768,768]{1,0:T(8,128)(2,1)S(1)} %collective-permute-done.6.refs_2_), channel_id=1, source_target_pairs={{8,0},{16,8},{24,16},{28,24},{20,28},{12,20},{4,12},{0,4},{9,1},{1... | collective-permute-start | bytes 3538952 | tf_op jit(solution)/shard_map/ppermute | solution.py:183
  238.7 50.0 %collective-permute-start.13 = (bf16[768,768]{1,0:T(8,128)(2,1)}, bf16[768,768]{1,0:T(8,128)(2,1)}, u32[]{:S(2)}, u32[]{:S(2)}) collective-permute-start(bf16[768,768]{1,0:T(8,128)(2,1)} %collective-permute-done.7.refs_3_), channel_id=1, source_target_pairs={{0,8},{8,16},{16,24},{24,28},{28,20},{20,12},{12,4},{4,0},{1,9},{9... | collective-permute-start | bytes 3538952 | tf_op jit(solution)/shard_map/ppermute | solution.py:182
  261.9 50.0 %collective-permute-start.9 = (bf16[768,768]{1,0:T(8,128)(2,1)S(1)}, bf16[768,768]{1,0:T(8,128)(2,1)}, u32[]{:S(2)}, u32[]{:S(2)}) collective-permute-start(bf16[768,768]{1,0:T(8,128)(2,1)S(1)} %collective-permute-done.5.refs_1_), channel_id=1, source_target_pairs={{0,8},{8,16},{16,24},{24,28},{28,20},{20,12},{12,4},{4,0},{1,9},{9... | collective-permute-start | bytes 3538952 | tf_op jit(solution)/shard_map/ppermute | solution.py:182
  263.5 49.6 %collective-permute-start.11 = (bf16[768,768]{1,0:T(8,128)(2,1)}, bf16[768,768]{1,0:T(8,128)(2,1)}, u32[]{:S(2)}, u32[]{:S(2)}) collective-permute-start(bf16[768,768]{1,0:T(8,128)(2,1)} %collective-permute-done.10.refs_4_), channel_id=1, source_target_pairs={{8,0},{16,8},{24,16},{28,24},{20,28},{12,20},{4,12},{0,4},{9,1},{1... | collective-permute-start | bytes 3538952 | tf_op jit(solution)/shard_map/ppermute | solution.py:183
  329.6 68.0 %reduce-scatter.7.cloned.1.call-start = ((), (), s32[]{:S(2)}) async-start(), calls=%async_computation.8 | async-start | bytes 2949120
  365.8 35.7 %all-to-all-start.3 = ((bf16[8,192,384]{2,1,0:T(8,128)(2,1)}), bf16[8,192,384]{2,1,0:T(8,128)(2,1)S(1)}, u32[]{:S(2)}, u32[]{:S(2)}) async-start(bf16[8,192,384]{2,1,0:T(8,128)(2,1)} %bitcast.19), calls=%async_computation.3 | async-start | bytes 2359296 | tf_op jit(solution)/shard_map/all_to_all | solution.py:235
  401.5 34.3 %all-to-all-start.2 = ((bf16[8,192,384]{2,1,0:T(8,128)(2,1)}), bf16[8,192,384]{2,1,0:T(8,128)(2,1)}, u32[]{:S(2)}, u32[]{:S(2)}) async-start(bf16[8,192,384]{2,1,0:T(8,128)(2,1)} %bitcast.17), calls=%async_computation.2 | async-start | bytes 2359296 | tf_op jit(solution)/shard_map/all_to_all | solution.py:235
  (17 other events, 302.3 us)
Sparse Core Ops, SparseCore 0:
  52.0 23.1 all-gather.4
  88.4 22.7 all-gather.6
  329.7 32.1 reduce-scatter.8
  364.4 33.0 reduce-scatter.6

commit v3 on v2

--- a/solution.py
+++ b/solution.py
@@ -263,15 +263,19 @@
     picker = ((jnp.arange(half)[None, :] == slot_index[:, None]) & slot_used[:, None]).astype(
         jnp.bfloat16
     )
-    w_parts = w_out.reshape(w_out.shape[0], parts, chunks, piece)
     shares = [
         lax.psum_scatter(
-            lax.dot_general(
-                w_parts[:, :, c].reshape(w_out.shape[0], parts * piece),
-                attended,
-                (((0,), (1,)), ((), ())),
-                preferred_element_type=jnp.float32,
-            ).astype(jnp.bfloat16),
+            jnp.concatenate(
+                [
+                    jnp.dot(
+                        attended,
+                        w_out[:, p * width + c * piece : p * width + (c + 1) * piece],
+                        preferred_element_type=jnp.float32,
+                    ).astype(jnp.bfloat16)
+                    for p in range(parts)
+                ],
+                axis=0,
+            ),
             "head",
             scatter_dimension=0,
             tiled=True,
@@ -281,7 +285,7 @@
     kept_out, moved_out = [], []
     for c in range(chunks):
         cols = slice(c * piece, (c + 1) * piece)
-        proj = shares[c].T
+        proj = shares[c]
         returning = jnp.dot(picker, proj, preferred_element_type=jnp.float32).astype(jnp.bfloat16)
         back = exchange(returning)
         kept_out.append(kept[:, cols].astype(jnp.float32) + gate_here[cols] * proj.astype(jnp.float32))

time: 448 us -> 448 us (level)
  local copies, waits for them, and re-layouts: 22.7 us -> 6.27 us
  waiting for transfers between devices: 205 us -> 212 us
  matrix products: 29.3 us -> 34.9 us
    unnamed x6 -> x4, waiting for transfers between devices: 52.3 us -> 0.07 us
    reduce_scatter x0 -> x2, waiting for transfers between devices: none -> 49.1 us  [body(): lax.psum_scatter(jnp.concatenate([jnp.dot(attended, w_out[:, p * width +...]
    unnamed x46 -> x37, local copies, waits for them, and re-layouts: 12.8 us -> 0.58 us
    ppermute x7, waiting for transfers between devices: 64.7 us -> 75.6 us  [attend(): move_left = lambda x: lax.ppermute(x, 'seq', left)]
    dot_general x2 -> x8, matrix products: 5.71 us -> 10.8 us  [body(): jnp.dot(attended, w_out[:, p * width + c * piece:p * width + (c + 1) * pi...]
  transfers between devices with their start and end apart: 21 -> 21, of which waited for: 14 -> 13; matrix products, arithmetic and copies ran while one was open for 11% -> 9% of each run, Pallas kernels for 14% -> 14%
where the time goes in v3:
time: 448 us; the launch traced here: 446 us
  waiting for transfers between devices  212 us (47%)
  Pallas kernels  96.6 us (22%)
  matrix products  34.9 us (8%)
  starting transfers between devices  33 us (7%)
  blocking collectives  32.5 us (7%)
  other arithmetic  17.5 us (4%)
  between operations  13.4 us (3%)
  local copies, waits for them, and re-layouts  6.27 us (1%)
    pallas_call x5, Pallas kernels, flash(): pl.pallas_call(functools.partial(flash_kernel, blocks, group, first, last...  75.9 us
    ppermute x7, waiting for transfers between devices, attend(): move_left = lambda x: lax.ppermute(x, 'seq', left)  75.6 us
    reduce_scatter x2, waiting for transfers between devices, body(): lax.psum_scatter(jnp.concatenate([jnp.dot(attended, w_out[:, p * width +...  49.1 us
    all_to_all x3, waiting for transfers between devices, exchange(): lax.all_to_all(x.reshape(shards, capacity, piece), 'seq', split_axis=0, c...  37.6 us
    all_to_all x1, blocking collectives, exchange(): lax.all_to_all(x.reshape(shards, capacity, piece), 'seq', split_axis=0, c...  32.5 us
    ppermute x7, waiting for transfers between devices, attend(): move_right = lambda x: lax.ppermute(x, 'seq', right)  27 us
    all_gather x2, waiting for transfers between devices, body(): gathered.append(lax.all_gather(merged, 'head', axis=0, tiled=False))  22.7 us
    pallas_call x1, Pallas kernels, project_qkv(): pl.pallas_call(functools.partial(qkv_kernel, len(gathered), group), grid=...  20.7 us
  transfers between devices with their start and end apart: 21, of which 13 were waited for; matrix products, arithmetic and copies ran while one was open for 9% of the time, Pallas kernels for 14%

profile of v3, /device:TPU:0, one launch (start us, length us, event | category | flops | bytes accessed | tf_op | source)
XLA Modules:
  0.0 446.3 jit_solution(4201909899178896065)
XLA Ops:
  9.4 3.5 fusion.18
  12.9 7.4 %all-to-all-start = ((bf16[8,192,384]{2,1,0:T(8,128)(2,1)}), bf16[8,192,384]{2,1,0:T(8,128)(2,1)S(1)}, u32[]{:S(2)}, u32[]{:S(2)}) async-start(bf16[8,192,384]{2,1,0:T(8,128)(2,1)} %bitcast), calls=%async_computation | async-start | bytes 2359296 | tf_op jit(solution)/shard_map/all_to_all | solution.py:235
  33.8 15.1 %all-to-all-done = bf16[8,192,384]{2,1,0:T(8,128)(2,1)S(1)} async-done(((bf16[8,192,384]{2,1,0:T(8,128)(2,1)}), bf16[8,192,384]{2,1,0:T(8,128)(2,1)S(1)}, u32[]{:S(2)}, u32[]{:S(2)}) %all-to-all-start) | async-done | bytes 1179680 | tf_op jit(solution)/shard_map/all_to_all | solution.py:235
  53.3 32.5 %all_to_all.20 = bf16[8,192,384]{2,1,0:T(8,128)(2,1)S(1)} all-to-all(bf16[8,192,384]{2,1,0:T(8,128)(2,1)S(1)} %bitcast.37), channel_id=1, replica_groups=mesh['seq'=8,'head'=4] {'seq'}, dimensions={0} | all-to-all | bytes 2359296 | tf_op jit(solution)/shard_map/all_to_all | solution.py:235
  88.5 22.6 %all-gather.7.cloned.1.call-done = bf16[3072,384]{1,0:T(8,128)(2,1)} async-done(((bf16[768,384]{1,0:T(8,128)(2,1)}), bf16[3072,384]{1,0:T(8,128)(2,1)}) %all-gather.7.cloned.1.call-update) | async-done | bytes 2359312 | tf_op jit(solution)/shard_map/all_gather | solution.py:259
  111.1 20.7 %shard_map.109 = (bf16[768,768]{1,0:T(8,128)(2,1)S(1)}, bf16[768,768]{1,0:T(8,128)(2,1)S(1)}, bf16[768,768]{1,0:T(8,128)(2,1)S(1)}) custom-call(bf16[4,768,384]{2,1,0:T(8,128)(2,1)} %bitcast.40, bf16[4,768,384]{2,1,0:T(8,128)(2,1)} %bitcast.41, bf16[3072,2304]{1,0:T(8,128)(2,1)} %refs_2_.1, f32[1,3072]{1,0:T(1,128)S(1)} %bitcast.29, f32[1,3072]{1,0:T(1,128)S(1)} %bitcast.30, ...), custom_call_target="tpu_custom_call" | custom-call | flops 10871635968 | bytes 33030144 | tf_op jit(solution)/shard_map/pallas_call | solution.py:74
  136.0 9.6 %shard_map.110 = (f32[768,768]{1,0:T(8,128)}, f32[768,1536]{1,0:T(8,128)}) custom-call(bf16[768,768]{1,0:T(8,128)(2,1)S(1)} %get-tuple-element.26.refs_0_, bf16[768,768]{1,0:T(8,128)(2,1)S(1)} %get-tuple-element.27.refs_1_, bf16[768,768]{1,0:T(8,128)(2,1)S(1)} %get-tuple-element.28.refs_2_), custom_call_target="tpu_custom_call" | custom-call | flops 3623878656 | bytes 11796480 | tf_op jit(solution)/shard_map/pallas_call | solution.py:151
  145.5 15.2 %collective-permute-done.refs_1_ = bf16[768,768]{1,0:T(8,128)(2,1)S(1)} collective-permute-done((bf16[768,768]{1,0:T(8,128)(2,1)S(1)}, bf16[768,768]{1,0:T(8,128)(2,1)S(1)}, u32[]{:S(2)}, u32[]{:S(2)}) %collective-permute-start) | collective-permute-done | bytes 1179680 | tf_op jit(solution)/shard_map/ppermute | solution.py:182
  162.8 24.7 %collective-permute-done.2.refs_2_ = bf16[768,768]{1,0:T(8,128)(2,1)S(1)} collective-permute-done((bf16[768,768]{1,0:T(8,128)(2,1)S(1)}, bf16[768,768]{1,0:T(8,128)(2,1)S(1)}, u32[]{:S(2)}, u32[]{:S(2)}) %collective-permute-start.2) | collective-permute-done | bytes 1179680 | tf_op jit(solution)/shard_map/ppermute | solution.py:183
  189.6 18.1 %shard_map.111 = (f32[768,768]{1,0:T(8,128)}, f32[768,1536]{1,0:T(8,128)}) custom-call(bf16[768,768]{1,0:T(8,128)(2,1)S(1)} %get-tuple-element.26.refs_0_, bf16[768,768]{1,0:T(8,128)(2,1)S(1)} %collective-permute-done.refs_1_, bf16[768,768]{1,0:T(8,128)(2,1)S(1)} %collective-permute-done.2.refs_2_, bf16[768,768]{1,0:T(8,128)(2,1)} %copy-done.12, ...), custom_call_target="tpu_custom_call" | custom-call | flops 7247757312 | bytes 14155776 | tf_op jit(solution)/shard_map/pallas_call | solution.py:151
  207.7 3.6 collective-permute-done.1.refs_1_
  213.4 24.7 %collective-permute-done.6.refs_2_ = bf16[768,768]{1,0:T(8,128)(2,1)S(1)} collective-permute-done((bf16[768,768]{1,0:T(8,128)(2,1)S(1)}, bf16[768,768]{1,0:T(8,128)(2,1)S(1)}, u32[]{:S(2)}, u32[]{:S(2)}) %collective-permute-start.6) | collective-permute-done | bytes 1179680 | tf_op jit(solution)/shard_map/ppermute | solution.py:183
  240.1 18.3 %shard_map.112 = (f32[768,768]{1,0:T(8,128)}, f32[768,1536]{1,0:T(8,128)}) custom-call(bf16[768,768]{1,0:T(8,128)(2,1)S(1)} %get-tuple-element.26.refs_0_, bf16[768,768]{1,0:T(8,128)(2,1)S(1)} %collective-permute-done.1.refs_1_, bf16[768,768]{1,0:T(8,128)(2,1)S(1)} %collective-permute-done.6.refs_2_, bf16[768,768]{1,0:T(8,128)(2,1)} %copy-done.13, ...), custom_call_target="tpu_custom_call" | custom-call | flops 7247757312 | bytes 14155776 | tf_op jit(solution)/shard_map/pallas_call | solution.py:151
  263.9 24.7 %collective-permute-done.12.refs_2_ = bf16[768,768]{1,0:T(8,128)(2,1)S(1)} collective-permute-done((bf16[768,768]{1,0:T(8,128)(2,1)S(1)}, bf16[768,768]{1,0:T(8,128)(2,1)S(1)}, u32[]{:S(2)}, u32[]{:S(2)}) %collective-permute-start.12) | collective-permute-done | bytes 1179680 | tf_op jit(solution)/shard_map/ppermute | solution.py:183
  288.7 18.2 %shard_map.113 = (f32[768,768]{1,0:T(8,128)}, f32[768,1536]{1,0:T(8,128)}) custom-call(bf16[768,768]{1,0:T(8,128)(2,1)S(1)} %get-tuple-element.26.refs_0_, bf16[768,768]{1,0:T(8,128)(2,1)S(1)} %collective-permute-done.5.refs_1_, bf16[768,768]{1,0:T(8,128)(2,1)S(1)} %collective-permute-done.12.refs_2_, bf16[768,768]{1,0:T(8,128)(2,1)} %collective-permute-done.13.refs_3_, ...), custom_call_target="tpu_custom_call" | custom-call | flops 7247757312 | bytes 14155776 | tf_op jit(solution)/shard_map/pallas_call | solution.py:151
  306.8 4.9 %collective-permute-done.9.refs_1_ = bf16[768,768]{1,0:T(8,128)(2,1)S(1)} collective-permute-done((bf16[768,768]{1,0:T(8,128)(2,1)S(1)}, bf16[768,768]{1,0:T(8,128)(2,1)S(1)}, u32[]{:S(2)}, u32[]{:S(2)}) %collective-permute-start.9) | collective-permute-done | bytes 1179680 | tf_op jit(solution)/shard_map/ppermute | solution.py:182
  313.0 11.7 %shard_map.114 = bf16[768,768]{1,0:T(8,128)(2,1)S(1)} custom-call(bf16[768,768]{1,0:T(8,128)(2,1)S(1)} %get-tuple-element.26.refs_0_, bf16[768,768]{1,0:T(8,128)(2,1)S(1)} %collective-permute-done.9.refs_1_, bf16[768,768]{1,0:T(8,128)(2,1)} %collective-permute-done.11.refs_2_, f32[768,768]{1,0:T(8,128)} %get-tuple-element.45.refs_3_, ...), custom_call_target="tpu_custom_call" | custom-call | flops 3623878656 | bytes 11796480 | tf_op jit(solution)/shard_map/pallas_call | solution.py:151
  339.0 22.9 %reduce-scatter.5.cloned.1.call-done = bf16[768,384]{1,0:T(8,128)(2,1)} async-done(((bf16[3072,384]{1,0:T(8,128)(2,1)}), bf16[768,384]{1,0:T(8,128)(2,1)}) %reduce-scatter.5.cloned.1.call-update) | async-done | bytes 589840 | tf_op jit(solution)/shard_map/reduce_scatter | solution.py:267
  361.9 4.0 fusion.15
  365.8 5.5 %all-to-all-start.3 = ((bf16[8,192,384]{2,1,0:T(8,128)(2,1)}), bf16[8,192,384]{2,1,0:T(8,128)(2,1)S(1)}, u32[]{:S(2)}, u32[]{:S(2)}) async-start(bf16[8,192,384]{2,1,0:T(8,128)(2,1)} %bitcast.12), calls=%async_computation.5 | async-start | bytes 2359296 | tf_op jit(solution)/shard_map/all_to_all | solution.py:235
  371.3 26.2 %reduce-scatter.3.cloned.1.call-done = bf16[768,384]{1,0:T(8,128)(2,1)} async-done(((bf16[3072,384]{1,0:T(8,128)(2,1)}), bf16[768,384]{1,0:T(8,128)(2,1)}) %reduce-scatter.3.cloned.1.call-update) | async-done | bytes 589840 | tf_op jit(solution)/shard_map/reduce_scatter | solution.py:267
  397.5 4.0 fusion.12
  401.5 5.5 %all-to-all-start.2 = ((bf16[8,192,384]{2,1,0:T(8,128)(2,1)}), bf16[8,192,384]{2,1,0:T(8,128)(2,1)S(1)}, u32[]{:S(2)}, u32[]{:S(2)}) async-start(bf16[8,192,384]{2,1,0:T(8,128)(2,1)} %bitcast.10), calls=%async_computation.4 | async-start | bytes 2359296 | tf_op jit(solution)/shard_map/all_to_all | solution.py:235
  413.1 22.5 %all-to-all-done.2 = bf16[8,192,384]{2,1,0:T(8,128)(2,1)S(1)} async-done(((bf16[8,192,384]{2,1,0:T(8,128)(2,1)}), bf16[8,192,384]{2,1,0:T(8,128)(2,1)S(1)}, u32[]{:S(2)}, u32[]{:S(2)}) %all-to-all-start.2) | async-done | bytes 1179680 | tf_op jit(solution)/shard_map/all_to_all | solution.py:235
  (106 shorter events, 66.8 us)
Async XLA Ops:
  12.9 36.0 %copy-start.5 = (bf16[1536,768]{1,0:T(8,128)(2,1)S(1)}, bf16[1536,768]{1,0:T(8,128)(2,1)}, u32[]{:S(2)}) copy-start(bf16[1536,768]{1,0:T(8,128)(2,1)} %param.11) | copy-start | bytes 7077892
  12.9 36.0 %all-to-all-start = ((bf16[8,192,384]{2,1,0:T(8,128)(2,1)}), bf16[8,192,384]{2,1,0:T(8,128)(2,1)S(1)}, u32[]{:S(2)}, u32[]{:S(2)}) async-start(bf16[8,192,384]{2,1,0:T(8,128)(2,1)} %bitcast), calls=%async_computation | async-start | bytes 2359296 | tf_op jit(solution)/shard_map/all_to_all | solution.py:235
  20.3 68.1 %all-gather.5.cloned.1.call-start = ((), (), s32[]{:S(2)}) async-start(), calls=%async_computation.8 | async-start | bytes 2949120 | tf_op jit(solution)/shard_map/all_gather | solution.py:259
  51.9 59.2 %all-gather.7.cloned.1.call-start = ((), (), s32[]{:S(2)}) async-start(), calls=%async_computation.9 | async-start | bytes 2949120 | tf_op jit(solution)/shard_map/all_gather | solution.py:259
  88.2 273.7 %reduce-scatter.5.cloned.1.call-start = ((), (), s32[]{:S(2)}) async-start(), calls=%async_computation.7 | async-start | bytes 2949120 | tf_op jit(solution)/shard_map/reduce_scatter | solution.py:267
  131.9 28.9 %collective-permute-start = (bf16[768,768]{1,0:T(8,128)(2,1)S(1)}, bf16[768,768]{1,0:T(8,128)(2,1)S(1)}, u32[]{:S(2)}, u32[]{:S(2)}) collective-permute-start(bf16[768,768]{1,0:T(8,128)(2,1)S(1)} %get-tuple-element.27.refs_1_), channel_id=1, source_target_pairs={{0,8},{8,16},{16,24},{24,28},{28,20},{20,12},{12,4},{4,0},{1,9},{9... | collective-permute-start | bytes 3538952 | tf_op jit(solution)/shard_map/ppermute | solution.py:182
  133.4 28.8 %collective-permute-start.4 = (bf16[768,768]{1,0:T(8,128)(2,1)S(1)}, bf16[768,768]{1,0:T(8,128)(2,1)S(1)}, u32[]{:S(2)}, u32[]{:S(2)}) collective-permute-start(bf16[768,768]{1,0:T(8,128)(2,1)S(1)} %get-tuple-element.28.refs_2_), channel_id=1, source_target_pairs={{8,0},{16,8},{24,16},{28,24},{20,28},{12,20},{4,12},{0,4},{9,1},{1... | collective-permute-start | bytes 3538952 | tf_op jit(solution)/shard_map/ppermute | solution.py:183
  133.9 53.6 %collective-permute-start.2 = (bf16[768,768]{1,0:T(8,128)(2,1)S(1)}, bf16[768,768]{1,0:T(8,128)(2,1)S(1)}, u32[]{:S(2)}, u32[]{:S(2)}) collective-permute-start(bf16[768,768]{1,0:T(8,128)(2,1)S(1)} %get-tuple-element.27.refs_1_), channel_id=1, source_target_pairs={{8,0},{16,8},{24,16},{28,24},{20,28},{12,20},{4,12},{0,4},{9,1},{1... | collective-permute-start | bytes 3538952 | tf_op jit(solution)/shard_map/ppermute | solution.py:183
  135.4 52.7 %collective-permute-start.3 = (bf16[768,768]{1,0:T(8,128)(2,1)S(1)}, bf16[768,768]{1,0:T(8,128)(2,1)S(1)}, u32[]{:S(2)}, u32[]{:S(2)}) collective-permute-start(bf16[768,768]{1,0:T(8,128)(2,1)S(1)} %get-tuple-element.28.refs_2_), channel_id=1, source_target_pairs={{0,8},{8,16},{16,24},{24,28},{28,20},{20,12},{12,4},{4,0},{1,9},{9... | collective-permute-start | bytes 3538952 | tf_op jit(solution)/shard_map/ppermute | solution.py:182
  160.7 50.6 %collective-permute-start.1 = (bf16[768,768]{1,0:T(8,128)(2,1)S(1)}, bf16[768,768]{1,0:T(8,128)(2,1)S(1)}, u32[]{:S(2)}, u32[]{:S(2)}) collective-permute-start(bf16[768,768]{1,0:T(8,128)(2,1)S(1)} %collective-permute-done.refs_1_), channel_id=1, source_target_pairs={{0,8},{8,16},{16,24},{24,28},{28,20},{20,12},{12,4},{4,0},{1,9},{9... | collective-permute-start | bytes 3538952 | tf_op jit(solution)/shard_map/ppermute | solution.py:182
  162.3 50.6 %collective-permute-start.8 = (bf16[768,768]{1,0:T(8,128)(2,1)S(1)}, bf16[768,768]{1,0:T(8,128)(2,1)S(1)}, u32[]{:S(2)}, u32[]{:S(2)}) collective-permute-start(bf16[768,768]{1,0:T(8,128)(2,1)S(1)} %collective-permute-done.4.refs_4_), channel_id=1, source_target_pairs={{8,0},{16,8},{24,16},{28,24},{20,28},{12,20},{4,12},{0,4},{9,1},{1... | collective-permute-start | bytes 3538952 | tf_op jit(solution)/shard_map/ppermute | solution.py:183
  187.5 50.6 %collective-permute-start.6 = (bf16[768,768]{1,0:T(8,128)(2,1)S(1)}, bf16[768,768]{1,0:T(8,128)(2,1)S(1)}, u32[]{:S(2)}, u32[]{:S(2)}) collective-permute-start(bf16[768,768]{1,0:T(8,128)(2,1)S(1)} %collective-permute-done.2.refs_2_), channel_id=1, source_target_pairs={{8,0},{16,8},{24,16},{28,24},{20,28},{12,20},{4,12},{0,4},{9,1},{1... | collective-permute-start | bytes 3538952 | tf_op jit(solution)/shard_map/ppermute | solution.py:183
  188.1 50.6 %collective-permute-start.7 = (bf16[768,768]{1,0:T(8,128)(2,1)S(1)}, bf16[768,768]{1,0:T(8,128)(2,1)S(1)}, u32[]{:S(2)}, u32[]{:S(2)}) collective-permute-start(bf16[768,768]{1,0:T(8,128)(2,1)S(1)} %collective-permute-done.3.refs_3_), channel_id=1, source_target_pairs={{0,8},{8,16},{16,24},{24,28},{28,20},{20,12},{12,4},{4,0},{1,9},{9... | collective-permute-start | bytes 3538952 | tf_op jit(solution)/shard_map/ppermute | solution.py:182
  211.3 50.6 %collective-permute-start.5 = (bf16[768,768]{1,0:T(8,128)(2,1)S(1)}, bf16[768,768]{1,0:T(8,128)(2,1)S(1)}, u32[]{:S(2)}, u32[]{:S(2)}) collective-permute-start(bf16[768,768]{1,0:T(8,128)(2,1)S(1)} %collective-permute-done.1.refs_1_), channel_id=1, source_target_pairs={{0,8},{8,16},{16,24},{24,28},{28,20},{20,12},{12,4},{4,0},{1,9},{9... | collective-permute-start | bytes 3538952 | tf_op jit(solution)/shard_map/ppermute | solution.py:182
  212.8 50.6 %collective-permute-start.10 = (bf16[768,768]{1,0:T(8,128)(2,1)S(1)}, bf16[768,768]{1,0:T(8,128)(2,1)S(1)}, u32[]{:S(2)}, u32[]{:S(2)}) collective-permute-start(bf16[768,768]{1,0:T(8,128)(2,1)S(1)} %collective-permute-done.8.refs_4_), channel_id=1, source_target_pairs={{8,0},{16,8},{24,16},{28,24},{20,28},{12,20},{4,12},{0,4},{9,1},{1... | collective-permute-start | bytes 3538952 | tf_op jit(solution)/shard_map/ppermute | solution.py:183
  238.1 50.6 %collective-permute-start.12 = (bf16[768,768]{1,0:T(8,128)(2,1)S(1)}, bf16[768,768]{1,0:T(8,128)(2,1)S(1)}, u32[]{:S(2)}, u32[]{:S(2)}) collective-permute-start(bf16[768,768]{1,0:T(8,128)(2,1)S(1)} %collective-permute-done.6.refs_2_), channel_id=1, source_target_pairs={{8,0},{16,8},{24,16},{28,24},{20,28},{12,20},{4,12},{0,4},{9,1},{1... | collective-permute-start | bytes 3538952 | tf_op jit(solution)/shard_map/ppermute | solution.py:183
  238.6 50.0 %collective-permute-start.13 = (bf16[768,768]{1,0:T(8,128)(2,1)S(1)}, bf16[768,768]{1,0:T(8,128)(2,1)}, u32[]{:S(2)}, u32[]{:S(2)}) collective-permute-start(bf16[768,768]{1,0:T(8,128)(2,1)S(1)} %collective-permute-done.7.refs_3_), channel_id=1, source_target_pairs={{0,8},{8,16},{16,24},{24,28},{28,20},{20,12},{12,4},{4,0},{1,9},{9... | collective-permute-start | bytes 3538952 | tf_op jit(solution)/shard_map/ppermute | solution.py:182
  240.1 84.6 %slice-start = ((s8[4718592]{0:T(1024)(128)(4,1)}), s8[4194304]{0:T(1024)(128)(4,1)S(1)}, s32[]{:S(2)}) async-start(s8[4718592]{0:T(1024)(128)(4,1)} %bitcast.38), calls=%async_computation.10 | async-start | bytes 8388608
  261.8 49.9 %collective-permute-start.9 = (bf16[768,768]{1,0:T(8,128)(2,1)S(1)}, bf16[768,768]{1,0:T(8,128)(2,1)S(1)}, u32[]{:S(2)}, u32[]{:S(2)}) collective-permute-start(bf16[768,768]{1,0:T(8,128)(2,1)S(1)} %collective-permute-done.5.refs_1_), channel_id=1, source_target_pairs={{0,8},{8,16},{16,24},{24,28},{28,20},{20,12},{12,4},{4,0},{1,9},{9... | collective-permute-start | bytes 3538952 | tf_op jit(solution)/shard_map/ppermute | solution.py:182
  263.4 49.7 %collective-permute-start.11 = (bf16[768,768]{1,0:T(8,128)(2,1)S(1)}, bf16[768,768]{1,0:T(8,128)(2,1)}, u32[]{:S(2)}, u32[]{:S(2)}) collective-permute-start(bf16[768,768]{1,0:T(8,128)(2,1)S(1)} %collective-permute-done.10.refs_4_), channel_id=1, source_target_pairs={{8,0},{16,8},{24,16},{28,24},{20,28},{12,20},{4,12},{0,4},{9,1},{1... | collective-permute-start | bytes 3538952 | tf_op jit(solution)/shard_map/ppermute | solution.py:183
  288.7 36.1 %slice-start.1 = ((s8[4718592]{0:T(1024)(128)(4,1)}), s8[524288]{0:T(1024)(128)(4,1)S(1)}, s32[]{:S(2)}) async-start(s8[4718592]{0:T(1024)(128)(4,1)} %bitcast.38), calls=%async_computation.11 | async-start | bytes 1048576
  329.6 68.0 %reduce-scatter.3.cloned.1.call-start = ((), (), s32[]{:S(2)}) async-start(), calls=%async_computation.6 | async-start | bytes 2949120 | tf_op jit(solution)/shard_map/reduce_scatter | solution.py:267
  365.8 35.7 %all-to-all-start.3 = ((bf16[8,192,384]{2,1,0:T(8,128)(2,1)}), bf16[8,192,384]{2,1,0:T(8,128)(2,1)S(1)}, u32[]{:S(2)}, u32[]{:S(2)}) async-start(bf16[8,192,384]{2,1,0:T(8,128)(2,1)} %bitcast.12), calls=%async_computation.5 | async-start | bytes 2359296 | tf_op jit(solution)/shard_map/all_to_all | solution.py:235
  401.5 34.1 %all-to-all-start.2 = ((bf16[8,192,384]{2,1,0:T(8,128)(2,1)}), bf16[8,192,384]{2,1,0:T(8,128)(2,1)S(1)}, u32[]{:S(2)}, u32[]{:S(2)}) async-start(bf16[8,192,384]{2,1,0:T(8,128)(2,1)} %bitcast.10), calls=%async_computation.4 | async-start | bytes 2359296 | tf_op jit(solution)/shard_map/all_to_all | solution.py:235
  (15 other events, 259.9 us)
Sparse Core Ops, SparseCore 0:
  52.0 23.1 all-gather.4
  88.3 22.7 all-gather.6
  329.7 32.1 reduce-scatter.4
  364.4 33.0 reduce-scatter.2
